TPU v7x, 128 devices: a whole 4x4x4 slice. The times are simulated.
128 devices in a mesh: dp: 4 (over x), slab: 32 (over z, y, core).
Axes of the slice: x: 4, y: 4, z: 4, core: 2. Of those that a mesh axis runs over, the one named last changes fastest.
Arguments:
- features: bfloat16 [4, 32, 4, 16, 16, 1024], P('dp', 'slab'), may hold values from -6 to 6
- target: float32 [4, 32, 4, 16, 256], P('dp', 'slab'), may hold values from -6 to 6
- block_coords: int32 [4, 32, 4, 2], P('dp', 'slab'), may hold values from -1 to 15, as said below
- neighbours: int32 [4, 32, 4, 6], P('dp', 'slab'), may hold values from -1 to 3, as said below
- owners: int32 [4, 32, 4, 2], P('dp', 'slab'), may hold values from -1 to 31, as said below
- coarse_weight: bfloat16 [27, 4096], replicated, may hold values from -0.15625 to 0.15625
- decoder_weight: bfloat16 [27, 64], replicated, may hold values from -0.15625 to 0.15625
Outputs:
- residual: float32 [4, 32, 4, 16, 256], P('dp', 'slab')
- grad_coarse: float32 [27, 4096], P(None, 'slab')
- grad_decoder: float32 [27, 64], replicated
Inputs may be any that keep to these rules, and one draw needn't show every extreme that they name: `block_coords`: for an occupied slot the (x, y) block position on a 16 x 16 grid of the slab, distinct within a slab; (-1, -1) marks an empty slot. Empty slots lie anywhere in the list; in every draw some slab's list has no empty slot. In every tomogram one block position is occupied in every slab. `neighbours`: for an occupied slot of slab s, the list slots of the occupied blocks sharing its -z face (in slab s - 1, same position), +z face (in slab s + 1), and its -y, +y, -x, +x faces (in slab s, position changed by one); -1 where there is no such block, and all -1 for an empty slot. The relation is symmetric and agrees with block_coords. `owners`: A coarse block covers 2 x 2 fine block positions in x and y over the slabs 2j and 2j + 1 of a tomogram; an occupied fine block names (owner slab, owner slot) of its coarse block, the owner being a slab of the same tomogram. All fine blocks of a coarse block name the same pair, no two coarse blocks do, and each slab of a tomogram owns exactly 1 coarse blocks, in slots 0 to 0. One slab names one owner at most 2 times, and some slab names some owner exactly 2 times. (-1, -1) for an empty slot.
All inputs are finite; a program needn't handle non-finite values.
Results may differ from a plain program's by a relative error of at most 0.003.
The roundings to bfloat16 on the way count: a program that leaves them out, or rounds other values in their place, can miss the bound.
Values may be sent and summed in bfloat16 or wider, within the bound.
A program may use at most 192 MiB of HBM per device.

v0:
```python
import jax
import jax.numpy as jnp
from jax import lax
from jax.sharding import PartitionSpec as P

CCAP = 1


def with_halo(block, sides, width):
    for axis, dim in sides:
        count = lax.axis_size(axis)
        forward = [(i, i + 1) for i in range(count - 1)]
        backward = [(target, source) for source, target in forward]
        low = lax.ppermute(
            lax.slice_in_dim(block, block.shape[dim] - width, None, axis=dim), axis, forward
        )
        high = lax.ppermute(lax.slice_in_dim(block, 0, width, axis=dim), axis, backward)
        block = jnp.concatenate([low, block, high], axis=dim)
    return block


def take_planes(planes, picked):
    safe_index = jnp.maximum(picked, 0)
    fetched = jnp.take(planes, safe_index, axis=0)
    keep_mask = (picked >= 0).reshape((-1,) + (1,) * (planes.ndim - 1))
    return jnp.where(keep_mask, fetched, jnp.zeros_like(fetched))


def frame_blocks(volume, below_rim, above_rim, link_ids, plane_width):
    sectioned = jnp.concatenate(
        [
            take_planes(below_rim, link_ids[:, 0])[:, None],
            volume,
            take_planes(above_rim, link_ids[:, 1])[:, None],
        ],
        axis=1,
    )
    lower_side = take_planes(sectioned[:, :, -1], link_ids[:, 2])
    upper_side = take_planes(sectioned[:, :, 0], link_ids[:, 3])
    sectioned = jnp.concatenate([lower_side[:, :, None], sectioned, upper_side[:, :, None]], axis=2)
    lower_side = take_planes(sectioned[:, :, :, -plane_width:], link_ids[:, 4])
    upper_side = take_planes(sectioned[:, :, :, :plane_width], link_ids[:, 5])
    return jnp.concatenate([lower_side, sectioned, upper_side], axis=3)


def pool_mean(values, half_edge, channels):
    count_blocks = values.shape[0]
    grouped = values.astype(jnp.float32).reshape(
        count_blocks, half_edge, 2, half_edge, 2, half_edge, 2, channels
    )
    return grouped.mean(axis=(2, 4, 6)).reshape(
        count_blocks, half_edge, half_edge, half_edge * channels
    )


def pool_sum(values, count_blocks, half_edge, channels):
    grouped = values.reshape(count_blocks, half_edge, 2, half_edge, 2, half_edge, 2, channels)
    return grouped.sum(axis=(2, 4, 6)).reshape(
        count_blocks, half_edge, half_edge, half_edge * channels
    )


def upsample(octants, half_edge, channels):
    count_blocks = octants.shape[0]
    expanded = jnp.broadcast_to(
        octants.reshape(count_blocks, half_edge, 1, half_edge, 1, half_edge, 1, channels),
        (count_blocks, half_edge, 2, half_edge, 2, half_edge, 2, channels),
    )
    return expanded.reshape(count_blocks, 2 * half_edge, 2 * half_edge, 2 * half_edge * channels)


def octants_to_blocks(octants, count_coarse, half_edge, channels):
    grouped = octants.reshape(count_coarse, 2, 2, 2, half_edge, half_edge, half_edge, channels)
    return grouped.transpose(0, 1, 4, 2, 5, 3, 6, 7).reshape(
        count_coarse, 2 * half_edge, 2 * half_edge, 2 * half_edge * channels
    )


def blocks_to_octants(blocks, half_edge, channels):
    count_coarse = blocks.shape[0]
    grouped = blocks.reshape(count_coarse, 2, half_edge, 2, half_edge, 2, half_edge, channels)
    return grouped.transpose(0, 1, 3, 5, 2, 4, 6, 7).reshape(
        count_coarse * 8, half_edge, half_edge, half_edge * channels
    )


def coarse_patch(framed, step_z, step_y, block_edge, channels):
    window = framed[:, step_z : step_z + block_edge, step_y : step_y + block_edge, :]
    pieces = [
        window[..., step_x * channels : (step_x + block_edge) * channels].reshape(-1, channels)
        for step_x in range(3)
    ]
    return jnp.concatenate(pieces, axis=1)


def coarse_forward(framed, kernel_rows, block_edge, channels):
    summed = jnp.zeros((framed.shape[0] * block_edge**3, channels), jnp.float32)
    for step_z in range(3):
        for step_y in range(3):
            patch = coarse_patch(framed, step_z, step_y, block_edge, channels)
            summed = summed + jnp.dot(
                patch, kernel_rows[3 * step_z + step_y], preferred_element_type=jnp.float32
            )
    return summed


def coarse_kernel_grad(framed, cotangent, block_edge, channels):
    terms = []
    for step_z in range(3):
        for step_y in range(3):
            patch = coarse_patch(framed, step_z, step_y, block_edge, channels)
            terms.append(
                lax.dot_general(
                    patch, cotangent, (((0,), (0,)), ((), ())), preferred_element_type=jnp.float32
                )
            )
    return jnp.stack(terms)


def tap_selector(block_edge, flipped):
    tap_ids = jnp.arange(3, dtype=jnp.int32)[:, None, None]
    frame_ids = jnp.arange(block_edge + 2, dtype=jnp.int32)[None, :, None]
    cell_ids = jnp.arange(block_edge, dtype=jnp.int32)[None, None, :]
    if flipped:
        return (cell_ids + 2 - frame_ids == tap_ids).astype(jnp.float32)
    return (frame_ids - cell_ids == tap_ids).astype(jnp.float32)


def decode_band(kernel, block_edge, channels):
    kernel_taps = kernel.reshape(3, 3, 3, channels)
    selector = tap_selector(block_edge, False).astype(jnp.bfloat16)
    band = jnp.einsum("dpx,zydc->zypcx", selector, kernel_taps, preferred_element_type=jnp.float32)
    return band.astype(jnp.bfloat16).reshape(3, 3, (block_edge + 2) * channels, block_edge)


def spread_band(kernel, block_edge, channels):
    kernel_taps = kernel.reshape(3, 3, 3, channels)
    selector = tap_selector(block_edge, True).astype(jnp.bfloat16)
    band = jnp.einsum("dpx,zydc->zypxc", selector, kernel_taps, preferred_element_type=jnp.float32)
    return band.astype(jnp.bfloat16).reshape(3, 3, block_edge + 2, block_edge * channels)


def decode(framed, band, block_edge):
    summed = jnp.zeros((framed.shape[0], block_edge, block_edge, block_edge), jnp.float32)
    for step_z in range(3):
        for step_y in range(3):
            window = framed[:, step_z : step_z + block_edge, step_y : step_y + block_edge, :]
            summed = summed + jnp.einsum(
                "bzyr,rx->bzyx", window, band[step_z, step_y], preferred_element_type=jnp.float32
            )
    return summed


def kernel_term(framed, cotangent, block_edge, channels):
    selector = tap_selector(block_edge, False)
    terms = []
    for step_z in range(3):
        for step_y in range(3):
            window = framed[:, step_z : step_z + block_edge, step_y : step_y + block_edge, :]
            crossed = jnp.einsum(
                "bzyr,bzyx->rx", window, cotangent, preferred_element_type=jnp.float32
            )
            crossed = crossed.reshape(block_edge + 2, channels, block_edge)
            terms.append(
                jnp.einsum(
                    "dpx,pcx->dc",
                    selector,
                    crossed,
                    precision=lax.Precision.HIGHEST,
                    preferred_element_type=jnp.float32,
                )
            )
    return jnp.stack(terms).reshape(27, channels)


def spread_pooled(framed_cot, band, block_edge, half_edge, channels):
    count_blocks = framed_cot.shape[0]
    summed = jnp.zeros((count_blocks, block_edge, block_edge, block_edge * channels), jnp.float32)
    for step_z in range(3):
        for step_y in range(3):
            window = framed_cot[
                :, 2 - step_z : 2 - step_z + block_edge, 2 - step_y : 2 - step_y + block_edge, :
            ]
            summed = summed + jnp.einsum(
                "bzyp,pq->bzyq", window, band[step_z, step_y], preferred_element_type=jnp.float32
            )
    return pool_sum(summed, count_blocks, half_edge, channels)


def per_device(features, target, block_coords, neighbours, owners, coarse_weight, decoder_weight):
    fine_feat = features[0, 0]
    blocks_here = fine_feat.shape[0]
    block_edge = fine_feat.shape[1]
    channels = decoder_weight.shape[1]
    half_edge = block_edge // 2
    slab_count = lax.axis_size("slab")
    send_cap = max(-(-4 * CCAP // slab_count), 2 * -(-2 * CCAP // slab_count))
    send_rows = slab_count * send_cap
    coords_here = block_coords[0, 0]
    link_ids = neighbours[0, 0]
    owner_here = owners[0, 0]
    live_slot = owner_here[:, 0] >= 0
    live_cells = live_slot[:, None, None, None]
    pooled = jnp.where(live_cells, pool_mean(fine_feat, half_edge, channels), 0.0).astype(
        jnp.bfloat16
    )
    octant_code = (
        owner_here[:, 1] * 8
        + lax.axis_index("slab") % 2 * 4
        + coords_here[:, 1] % 2 * 2
        + coords_here[:, 0] % 2
    )
    slot_ids = jnp.arange(blocks_here, dtype=jnp.int32)
    earlier = (
        (owner_here[:, 0][:, None] == owner_here[:, 0][None, :])
        & live_slot[None, :]
        & (slot_ids[None, :] < slot_ids[:, None])
    )
    send_slot = jnp.where(live_slot, owner_here[:, 0] * send_cap + jnp.sum(earlier, axis=1), -1)
    placement = jnp.arange(send_rows, dtype=jnp.int32)[:, None] == send_slot[None, :]
    place_matrix = placement.astype(jnp.bfloat16)
    outgoing = jnp.dot(
        place_matrix, pooled.reshape(blocks_here, -1), preferred_element_type=jnp.float32
    ).astype(jnp.bfloat16)
    outgoing_code = jnp.sum(jnp.where(placement, octant_code[None, :] + 1, 0), axis=1).astype(
        jnp.bfloat16
    )
    arrived, arrived_code = (
        lax.all_to_all(
            outgoing.reshape(slab_count, send_cap, -1),
            "slab",
            split_axis=0,
            concat_axis=0,
            tiled=True,
        ),
        lax.all_to_all(
            outgoing_code.reshape(slab_count, send_cap),
            "slab",
            split_axis=0,
            concat_axis=0,
            tiled=True,
        ),
    )
    arrived = arrived.reshape(send_rows, -1)
    arrived_code = arrived_code.reshape(send_rows).astype(jnp.int32) - 1
    assemble = (jnp.arange(CCAP * 8, dtype=jnp.int32)[:, None] == arrived_code[None, :]).astype(
        jnp.bfloat16
    )
    coarse_oct = jnp.dot(assemble, arrived, preferred_element_type=jnp.float32).astype(jnp.bfloat16)
    coarse_in = octants_to_blocks(coarse_oct, CCAP, half_edge, channels)
    coarse_framed = jnp.pad(coarse_in, ((0, 0), (1, 1), (1, 1), (channels, channels)))
    kernel_rows = coarse_weight.reshape(9, 3 * channels, channels)
    coarse_pre = coarse_forward(coarse_framed, kernel_rows, block_edge, channels)
    coarse_out = (
        jnp.maximum(coarse_pre, 0.0)
        .astype(jnp.bfloat16)
        .reshape(CCAP, block_edge, block_edge, block_edge * channels)
    )
    back_items = jnp.dot(
        assemble.T,
        blocks_to_octants(coarse_out, half_edge, channels).reshape(CCAP * 8, -1),
        preferred_element_type=jnp.float32,
    ).astype(jnp.bfloat16)
    returned = lax.all_to_all(
        back_items.reshape(slab_count, send_cap, -1),
        "slab",
        split_axis=0,
        concat_axis=0,
        tiled=True,
    ).reshape(send_rows, -1)
    upward = jnp.dot(place_matrix.T, returned, preferred_element_type=jnp.float32).astype(
        jnp.bfloat16
    )
    upward = upward.reshape(blocks_here, half_edge, half_edge, half_edge * channels)
    mixed = jnp.where(
        live_cells,
        fine_feat.astype(jnp.float32) + upsample(upward, half_edge, channels).astype(jnp.float32),
        0.0,
    ).astype(jnp.bfloat16)
    rim_planes = with_halo(jnp.stack([mixed[:, 0], mixed[:, -1]], axis=1), (("slab", 1),), 1)
    framed_mix = frame_blocks(mixed, rim_planes[:, 0], rim_planes[:, 3], link_ids, channels)
    out_band = decode_band(decoder_weight, block_edge, channels)
    back_band = spread_band(decoder_weight, block_edge, channels)
    predicted = decode(framed_mix, out_band, block_edge)
    measured = target[0, 0].reshape(blocks_here, block_edge, block_edge, block_edge)
    residual = jnp.where(live_cells, predicted - measured, 0.0)
    cotangent = (residual / (blocks_here * block_edge**3)).astype(jnp.bfloat16)
    decoder_term = kernel_term(framed_mix, cotangent, block_edge, channels)
    cot_planes = with_halo(
        jnp.stack([cotangent[:, 0], cotangent[:, -1]], axis=1), (("slab", 1),), 1
    )
    framed_cot = frame_blocks(cotangent, cot_planes[:, 0], cot_planes[:, 3], link_ids, 1)
    dupward = jnp.where(
        live_cells, spread_pooled(framed_cot, back_band, block_edge, half_edge, channels), 0.0
    ).astype(jnp.bfloat16)
    outgoing_cot = jnp.dot(
        place_matrix, dupward.reshape(blocks_here, -1), preferred_element_type=jnp.float32
    ).astype(jnp.bfloat16)
    arrived_cot = lax.all_to_all(
        outgoing_cot.reshape(slab_count, send_cap, -1),
        "slab",
        split_axis=0,
        concat_axis=0,
        tiled=True,
    ).reshape(send_rows, -1)
    dcoarse_oct = jnp.dot(assemble, arrived_cot, preferred_element_type=jnp.float32).astype(
        jnp.bfloat16
    )
    dcoarse = octants_to_blocks(dcoarse_oct, CCAP, half_edge, channels).reshape(-1, channels)
    dpre = jnp.where(coarse_pre > 0, dcoarse, jnp.zeros_like(dcoarse))
    coarse_term = coarse_kernel_grad(coarse_framed, dpre, block_edge, channels).reshape(
        27, channels * channels
    )
    coarse_total, decoder_total = lax.psum((coarse_term, decoder_term), ("dp", "slab"))
    share_width = coarse_total.shape[1] // slab_count
    coarse_mine = lax.dynamic_slice_in_dim(
        coarse_total, lax.axis_index("slab") * share_width, share_width, 1
    )
    residual_out = residual.reshape(1, 1, blocks_here, block_edge, block_edge * block_edge)
    return (residual_out, coarse_mine, decoder_total)


def solution(mesh):
    placed = (
        P("dp", "slab", None, None, None, None),
        P("dp", "slab", None, None, None),
        P("dp", "slab", None, None),
        P("dp", "slab", None, None),
        P("dp", "slab", None, None),
        P(),
        P(),
    )
    return jax.shard_map(
        per_device,
        mesh=mesh,
        in_specs=placed,
        out_specs=(P("dp", "slab", None, None, None), P(None, "slab"), P()),
        check_vma=False,
    )
```

profile of v0, /device:TPU:0, one launch (start us, length us, event | category | flops | bytes accessed | tf_op | source)
XLA Modules:
  0.0 685.3 jit_solution(1189003167092640719)
XLA Ops:
  10.3 8.4 %all-to-all-start = ((bf16[32,1,2]{2,1,0:T(2,128)(2,1)}), bf16[32,1,2]{2,1,0:T(2,128)(2,1)S(1)}, u32[]{:S(2)}, u32[]{:S(2)}) async-start(bf16[32,1,2]{2,1,0:T(2,128)(2,1)} %convert_element_type.149), calls=%async_computation | async-start | bytes 32768 | tf_op jit(solution)/shard_map/all_to_all | solution.py:236
  18.8 9.1 %reshape.535 = f32[4,8,2,8,2,8,2,64]{7,6,5,4,3,2,1,0:T(2,128)} reshape(bf16[1,1,4,16,16,1024]{5,4,3,2,1,0:T(8,128)(2,1)} %param.19) | data formatting | bytes 6291456 | tf_op jit(solution)/shard_map/convert_element_type | solution.py:277
  27.9 9.8 %reduce_sum.38 = f32[4,8,8,8,64]{4,3,2,1,0:T(8,128)S(1)} reduce(f32[4,8,2,8,2,8,2,64]{7,6,5,4,3,2,1,0:T(2,128)} %reshape.535, f32[]{:T(128)} %constant.76.clone.1), dimensions={2,4,6}, to_apply=%region_2.3 | reduce | flops 917504 | bytes 4718596 | tf_op jit(solution)/shard_map/reduce_sum | solution.py:51
  38.2 3.4 convolution_convert_fusion.2
  41.6 7.7 %reshape.481 = bf16[32,2,32768]{2,1,0:T(2,128)(2,1)} reshape(bf16[64,32768]{1,0:T(8,128)(2,1)} %convolution_convert_fusion.2) | data formatting | bytes 8388608 | tf_op jit(solution)/shard_map/reshape | solution.py:230
  49.3 7.8 %all-to-all-start.1 = ((bf16[32,2,32768]{2,1,0:T(2,128)(2,1)}), bf16[32,2,32768]{2,1,0:T(2,128)(2,1)}, u32[]{:S(2)}, u32[]{:S(2)}) async-start(bf16[32,2,32768]{2,1,0:T(2,128)(2,1)} %reshape.481), calls=%async_computation.1 | async-start | bytes 8388608 | tf_op jit(solution)/shard_map/all_to_all | solution.py:229
  59.0 51.6 %all-to-all-done.1 = bf16[32,2,32768]{2,1,0:T(2,128)(2,1)} async-done(((bf16[32,2,32768]{2,1,0:T(2,128)(2,1)}), bf16[32,2,32768]{2,1,0:T(2,128)(2,1)}, u32[]{:S(2)}, u32[]{:S(2)}) %all-to-all-start.1) | async-done | bytes 4194336 | tf_op jit(solution)/shard_map/all_to_all | solution.py:229
  110.6 7.3 %reshape.482 = bf16[64,32768]{1,0:T(8,128)(2,1)} reshape(bf16[32,2,32768]{2,1,0:T(2,128)(2,1)} %all-to-all-done.1) | data formatting | bytes 8388608 | tf_op jit(solution)/shard_map/reshape | solution.py:244
  117.9 2.8 convolution_convert_fusion.4
  122.8 3.4 pad_slice_fusion.1
  126.2 7.6 %pad_slice_fusion.2 = (bf16[1,16,16,1024]{3,2,1,0:T(8,128)(2,1)}, bf16[1,16,16,1024]{3,2,1,0:T(8,128)(2,1)}, bf16[1,16,16,1024]{3,2,1,0:T(8,128)(2,1)}, bf16[1,1...) fusion(bf16[1,16,16,1024]{3,2,1,0:T(8,128)(2,1)S(1)} %reshape.484), kind=kLoop, calls=%fused_computation.33 | loop fusion | bytes 10485760 | tf_op jit(solution)/shard_map/slice | solution.py:90
  133.8 2.6 reshape.510
  136.3 2.5 reshape.505
  138.8 2.5 reshape.506
  145.4 2.9 reshape.511
  148.4 2.5 reshape.485
  150.8 2.5 reshape.509
  153.4 2.5 reshape.486
  155.9 2.5 reshape.487
  160.0 2.5 reshape.489
  167.5 2.5 reshape.492
  170.0 2.5 reshape.493
  174.2 2.5 reshape.495
  176.7 2.5 reshape.496
  181.7 2.6 reshape.499
  184.3 2.5 reshape.500
  193.4 3.1 fusion.80
  212.9 3.3 convolution_convert_fusion.1
  216.2 7.7 %reshape.512 = bf16[32,2,32768]{2,1,0:T(2,128)(2,1)} reshape(bf16[64,32768]{1,0:T(8,128)(2,1)} %convolution_convert_fusion.1) | data formatting | bytes 8388608 | tf_op jit(solution)/shard_map/reshape | solution.py:265
  223.9 5.2 all-to-all-start.2
  235.3 47.3 %all-to-all-done.2 = bf16[32,2,32768]{2,1,0:T(2,128)(2,1)} async-done(((bf16[32,2,32768]{2,1,0:T(2,128)(2,1)}), bf16[32,2,32768]{2,1,0:T(2,128)(2,1)}, u32[]{:S(2)}, u32[]{:S(2)}) %all-to-all-start.2) | async-done | bytes 4194336 | tf_op jit(solution)/shard_map/all_to_all | solution.py:264
  282.6 7.3 %reshape.513 = bf16[64,32768]{1,0:T(8,128)(2,1)} reshape(bf16[32,2,32768]{2,1,0:T(2,128)(2,1)} %all-to-all-done.2) | data formatting | bytes 8388608 | tf_op jit(solution)/shard_map/reshape | solution.py:270
  289.8 2.9 fusion
  293.3 6.2 broadcast_in_dim.248
  299.5 10.7 %convert_element_type.132 = f32[4,16,16,1024]{3,2,1,0:T(8,128)} reshape(f32[4,8,2,8,2,8,2,64]{7,6,5,4,3,2,1,0:T(2,128)} %broadcast_in_dim.248) | data formatting | bytes 8388608 | tf_op jit(solution)/shard_map/convert_element_type | solution.py:277
  310.2 3.7 fusion.2
  329.2 2.6 pad_maximum_fusion
  334.7 2.8 gather_fusion.5
  337.5 2.5 gather_fusion.4
  343.9 7.4 %concatenate.65 = bf16[4,18,18,1152]{3,2,1,0:T(8,128)(2,1)} concatenate(bf16[4,18,18,64]{3,2,1,0:T(8,128)(2,1)} %select_select_fusion.3, bf16[4,18,18,1024]{3,2,1,0:T(8,128)(2,1)S(1)} %copy-done.1, bf16[4,18,18,64]{3,2,1,0:T(8,128)(2,1)} %select_select_fusion.2), dimensions={3} | concatenate | bytes 5971968 | tf_op jit(solution)/shard_map/concatenate | solution.py:43
  351.3 2.9 fusion.4
  361.4 3.0 collective-permute-start.2
  383.1 2.6 fusion.90
  385.7 2.7 fusion.92
  388.4 2.8 fusion.94
  391.2 2.7 fusion.96
  393.9 10.5 %add_add_fusion = f32[4,16,16,1024]{3,2,1,0:T(8,128)} fusion(f32[4,16,16,1024]{3,2,1,0:T(8,128)S(1)} %fusion.82, f32[4,16,16,1024]{3,2,1,0:T(8,128)S(1)} %fusion.84, f32[4,16,16,1024]{3,2,1,0:T(8,128)S(1)} %fusion.86, f32[4,16,16,1024]{3,2,1,0:T(8,128)S(1)} %fusion.88, f32[4,16,16,1024]{3,2,1,0:T(8,128)} %fusion.90, f32[4,16,16,1024]{3,2,1,0:T(8,128)} %fusion.92, ...), kind=kOutput, calls=%fused_computation.30 | convolution fusion | flops 46137344 | bytes 38060032 | tf_op jit(solution)/shard_map/bzyp,pq->bzyq/dot_general | solution.py:184
  404.4 10.2 %reshape.518 = f32[4,8,2,8,2,8,2,64]{7,6,5,4,3,2,1,0:T(2,128)} reshape(f32[4,16,16,1024]{3,2,1,0:T(8,128)} %add_add_fusion) | data formatting | bytes 8388608 | tf_op jit(solution)/shard_map/reshape | solution.py:57
  414.6 9.9 %reduce_sum.39 = bf16[4,8,8,8,64]{4,3,2,1,0:T(8,128)(2,1)S(1)} reduce(f32[4,8,2,8,2,8,2,64]{7,6,5,4,3,2,1,0:T(2,128)} %reshape.518, f32[]{:T(128)} %constant.76.clone.1), dimensions={2,4,6}, to_apply=%region_3.10 | reduce | flops 917504 | bytes 4456452 | tf_op jit(solution)/shard_map/reduce_sum | solution.py:58
  424.9 3.4 convolution_convert_fusion
  428.2 7.7 %reshape.520 = bf16[32,2,32768]{2,1,0:T(2,128)(2,1)} reshape(bf16[64,32768]{1,0:T(8,128)(2,1)} %convolution_convert_fusion) | data formatting | bytes 8388608 | tf_op jit(solution)/shard_map/reshape | solution.py:300
  435.9 11.9 %all-to-all-start.3 = ((bf16[32,2,32768]{2,1,0:T(2,128)(2,1)}), bf16[32,2,32768]{2,1,0:T(2,128)(2,1)}, u32[]{:S(2)}, u32[]{:S(2)}) async-start(bf16[32,2,32768]{2,1,0:T(2,128)(2,1)} %reshape.520), calls=%async_computation.3 | async-start | bytes 8388608 | tf_op jit(solution)/shard_map/all_to_all | solution.py:299
  448.1 2.8 convolution_bitcast_fusion.7
  450.9 2.8 convolution_bitcast_fusion.6
  456.0 2.8 convolution_bitcast_fusion.4
  458.9 2.8 convolution_bitcast_fusion.3
  464.0 2.8 convolution_bitcast_fusion.1
  466.9 2.8 convolution_bitcast_fusion
  472.5 28.8 %all-to-all-done.3 = bf16[32,2,32768]{2,1,0:T(2,128)(2,1)} async-done(((bf16[32,2,32768]{2,1,0:T(2,128)(2,1)}), bf16[32,2,32768]{2,1,0:T(2,128)(2,1)}, u32[]{:S(2)}, u32[]{:S(2)}) %all-to-all-start.3) | async-done | bytes 4194336 | tf_op jit(solution)/shard_map/all_to_all | solution.py:299
  501.3 7.3 %reshape.521 = bf16[64,32768]{1,0:T(8,128)(2,1)} reshape(bf16[32,2,32768]{2,1,0:T(2,128)(2,1)} %all-to-all-done.3) | data formatting | bytes 8388608 | tf_op jit(solution)/shard_map/reshape | solution.py:305
  508.6 2.8 convolution_convert_fusion.3
  514.7 3.3 fusion.70
  535.5 63.4 %psum.15 = f32[27,64]{1,0:T(8,128)} all-reduce(f32[27,64]{1,0:T(8,128)S(1)} %reshape.533), channel_id=1, replica_groups=mesh['dp'=4,'slab'=32] {'dp','slab'}, use_global_device_ids=true, to_apply=%region_5.12 | all-reduce | flops 1728 | bytes 13824 | tf_op jit(solution)/shard_map/psum | solution.py:314
  598.9 78.0 %all-reduce.3.cloned.1.call-done = f32[27,4096]{1,0:T(8,128)} async-done(((f32[27,4096]{1,0:T(8,128)}), f32[27,4096]{1,0:T(8,128)}) %all-reduce.3.cloned.1.call-update) | async-done | bytes 442384 | tf_op jit(solution)/shard_map/psum | solution.py:314
  (372 shorter events, 129.2 us)
Async XLA Ops:
  9.5 28.7 %copy-start.70 = (s32[4]{0:T(128)}, s32[4]{0:T(128)S(1)}, u32[]{:S(2)}) copy-start(s32[4]{0:T(128)S(1)} %get-tuple-element.80) | copy-start | bytes 52
  10.3 39.0 %all-to-all-start = ((bf16[32,1,2]{2,1,0:T(2,128)(2,1)}), bf16[32,1,2]{2,1,0:T(2,128)(2,1)S(1)}, u32[]{:S(2)}, u32[]{:S(2)}) async-start(bf16[32,1,2]{2,1,0:T(2,128)(2,1)} %convert_element_type.149), calls=%async_computation | async-start | bytes 32768 | tf_op jit(solution)/shard_map/all_to_all | solution.py:236
  49.3 7.8 %copy-start.59 = (bf16[27,4096]{1,0:T(8,128)(2,1)S(1)}, bf16[27,4096]{1,0:T(8,128)(2,1)}, u32[]{:S(2)}) copy-start(bf16[27,4096]{1,0:T(8,128)(2,1)} %param.24) | copy-start | bytes 663556
  49.3 61.3 %all-to-all-start.1 = ((bf16[32,2,32768]{2,1,0:T(2,128)(2,1)}), bf16[32,2,32768]{2,1,0:T(2,128)(2,1)}, u32[]{:S(2)}, u32[]{:S(2)}) async-start(bf16[32,2,32768]{2,1,0:T(2,128)(2,1)} %reshape.481), calls=%async_computation.1 | async-start | bytes 8388608 | tf_op jit(solution)/shard_map/all_to_all | solution.py:229
  122.1 79.6 %copy-start.3 = (bf16[1,2,2,2,8,8,8,64]{7,6,3,5,2,4,1,0:T(8,128)(2,1)}, bf16[1,2,2,2,8,8,8,64]{7,6,3,5,2,4,1,0:T(8,128)(2,1)S(1)}, u32[]{:S(2)}) copy-start(bf16[1,2,2,2,8,8,8,64]{7,6,3,5,2,4,1,0:T(8,128)(2,1)S(1)} %copy.283) | copy-start | bytes 1572868
  133.8 10.0 %copy-start.9 = (bf16[1,16,16,1024]{3,2,1,0:T(8,128)(2,1)S(1)}, bf16[1,16,16,1024]{3,2,1,0:T(8,128)(2,1)}, u32[]{:S(2)}) copy-start(bf16[1,16,16,1024]{3,2,1,0:T(8,128)(2,1)} %get-tuple-element.52) | copy-start | bytes 1572868
  145.4 13.0 %copy-start.7 = (bf16[1,16,16,1024]{3,2,1,0:T(8,128)(2,1)S(1)}, bf16[1,16,16,1024]{3,2,1,0:T(8,128)(2,1)}, u32[]{:S(2)}) copy-start(bf16[1,16,16,1024]{3,2,1,0:T(8,128)(2,1)} %get-tuple-element.32) | copy-start | bytes 1572868
  160.0 12.5 %copy-start.6 = (bf16[1,16,16,1024]{3,2,1,0:T(8,128)(2,1)S(1)}, bf16[1,16,16,1024]{3,2,1,0:T(8,128)(2,1)}, u32[]{:S(2)}) copy-start(bf16[1,16,16,1024]{3,2,1,0:T(8,128)(2,1)} %get-tuple-element.38) | copy-start | bytes 1572868
  174.2 12.6 %copy-start.5 = (bf16[1,16,16,1024]{3,2,1,0:T(8,128)(2,1)S(1)}, bf16[1,16,16,1024]{3,2,1,0:T(8,128)(2,1)}, u32[]{:S(2)}) copy-start(bf16[1,16,16,1024]{3,2,1,0:T(8,128)(2,1)} %get-tuple-element.44) | copy-start | bytes 1572868
  188.5 5.0 copy-start.69
  191.7 4.8 copy-start.26
  193.4 3.1 copy-start.28
  193.4 3.1 copy-start.32
  198.4 1.9 copy-start.52
  201.7 1.9 copy-start.54
  203.6 1.9 copy-start.56
  205.4 1.9 copy-start.19
  207.3 1.9 copy-start.23
  223.9 5.2 copy-start.73
  223.9 6.2 copy-start.60
  223.9 58.7 %all-to-all-start.2 = ((bf16[32,2,32768]{2,1,0:T(2,128)(2,1)}), bf16[32,2,32768]{2,1,0:T(2,128)(2,1)}, u32[]{:S(2)}, u32[]{:S(2)}) async-start(bf16[32,2,32768]{2,1,0:T(2,128)(2,1)} %reshape.512), calls=%async_computation.2 | async-start | bytes 8388608 | tf_op jit(solution)/shard_map/all_to_all | solution.py:264
  230.4 97.3 %copy-start.74 = (s32[1024]{0:T(1024)}, s32[1024]{0:T(1024)S(1)}, u32[]{:S(2)}) copy-start(s32[1024]{0:T(1024)S(1)} %pad_clamp_fusion.2) | copy-start | bytes 12292
  231.5 92.2 %copy-start.76 = (s32[1024]{0:T(1024)}, s32[1024]{0:T(1024)S(1)}, u32[]{:S(2)}) copy-start(s32[1024]{0:T(1024)S(1)} %pad_clamp_fusion.4) | copy-start | bytes 12292
  231.6 91.6 %copy-start.77 = (s32[1024]{0:T(1024)}, s32[1024]{0:T(1024)S(1)}, u32[]{:S(2)}) copy-start(s32[1024]{0:T(1024)S(1)} %pad_clamp_fusion.5) | copy-start | bytes 12292
  231.6 95.0 %copy-start.75 = (s32[1024]{0:T(1024)}, s32[1024]{0:T(1024)S(1)}, u32[]{:S(2)}) copy-start(s32[1024]{0:T(1024)S(1)} %pad_clamp_fusion.3) | copy-start | bytes 12292
  235.3 54.6 %copy-start.71 = (s32[4]{0:T(128)S(1)}, s32[4]{0:T(128)}, u32[]{:S(2)}) copy-start(s32[4]{0:T(128)} %copy-done.70) | copy-start | bytes 52
  310.2 6.4 copy-start.95
  314.0 9.2 %collective-permute-start = (bf16[4,1,16,1024]{3,2,1,0:T(8,128)(2,1)S(1)}, bf16[4,1,16,1024]{3,2,1,0:T(8,128)(2,1)S(1)}, u32[]{:S(2)}, u32[]{:S(2)}) collective-permute-start(bf16[4,1,16,1024]{3,2,1,0:T(8,128)(2,1)S(1)} %get-tuple-element.25), channel_id=1, source_target_pairs={{0,1},{1,2},{2,3},{3,4},{4,5},{5,6},{6,7},{7,8},{8,9},{9,10},{10,1... | collective-permute-start | bytes 393224 | tf_op jit(solution)/shard_map/ppermute | solution.py:14
  315.3 8.5 %collective-permute-start.1 = (bf16[4,1,16,1024]{3,2,1,0:T(8,128)(2,1)S(1)}, bf16[4,1,16,1024]{3,2,1,0:T(8,128)(2,1)S(1)}, u32[]{:S(2)}, u32[]{:S(2)}) collective-permute-start(bf16[4,1,16,1024]{3,2,1,0:T(8,128)(2,1)S(1)} %get-tuple-element.26), channel_id=1, source_target_pairs={{1,0},{2,1},{3,2},{4,3},{5,4},{6,5},{7,6},{8,7},{9,8},{10,9},{11,1... | collective-permute-start | bytes 393224 | tf_op jit(solution)/shard_map/ppermute | solution.py:17
  320.0 7.1 %copy-start.91 = (pred[4]{0:T(512)(128)(4,1)S(1)}, pred[4]{0:T(512)(128)(4,1)}, u32[]{:S(2)}) copy-start(pred[4]{0:T(512)(128)(4,1)} %get-tuple-element.92) | copy-start | bytes 16
  323.2 1.9 copy-start.86
  323.2 6.0 copy-start.80
  323.2 6.0 copy-start.82
  323.2 6.0 copy-start.84
  334.7 9.1 %copy-start.1 = (bf16[4,18,18,1024]{3,2,1,0:T(8,128)(2,1)S(1)}, bf16[4,18,18,1024]{3,2,1,0:T(8,128)(2,1)}, u32[]{:S(2)}) copy-start(bf16[4,18,18,1024]{3,2,1,0:T(8,128)(2,1)} %copy-done) | copy-start | bytes 7962628
  351.3 3.2 copy-start.2
  351.3 3.2 copy-start.68
  361.3 6.7 copy-start.87
  361.3 6.7 copy-start.94
  361.4 9.3 %copy-start.85 = (pred[4]{0:T(512)(128)(4,1)S(1)}, pred[4]{0:T(512)(128)(4,1)}, u32[]{:S(2)}) copy-start(pred[4]{0:T(512)(128)(4,1)} %copy-done.84) | copy-start | bytes 16
  361.4 9.3 %copy-start.93 = (pred[4]{0:T(512)(128)(4,1)S(1)}, pred[4]{0:T(512)(128)(4,1)}, u32[]{:S(2)}) copy-start(pred[4]{0:T(512)(128)(4,1)} %get-tuple-element.93) | copy-start | bytes 16
  361.4 10.3 %copy-start.83 = (pred[4]{0:T(512)(128)(4,1)S(1)}, pred[4]{0:T(512)(128)(4,1)}, u32[]{:S(2)}) copy-start(pred[4]{0:T(512)(128)(4,1)} %copy-done.82) | copy-start | bytes 16
  361.4 10.3 %copy-start.92 = (pred[4]{0:T(512)(128)(4,1)S(1)}, pred[4]{0:T(512)(128)(4,1)}, u32[]{:S(2)}) copy-start(pred[4]{0:T(512)(128)(4,1)} %get-tuple-element.92) | copy-start | bytes 16
  361.4 11.1 %copy-start.81 = (pred[4]{0:T(512)(128)(4,1)S(1)}, pred[4]{0:T(512)(128)(4,1)}, u32[]{:S(2)}) copy-start(pred[4]{0:T(512)(128)(4,1)} %copy-done.80) | copy-start | bytes 16
  361.4 11.1 %copy-start.90 = (pred[4]{0:T(512)(128)(4,1)S(1)}, pred[4]{0:T(512)(128)(4,1)}, u32[]{:S(2)}) copy-start(pred[4]{0:T(512)(128)(4,1)} %get-tuple-element.91) | copy-start | bytes 16
  361.4 15.0 %copy-start.79 = (pred[4]{0:T(512)(128)(4,1)S(1)}, pred[4]{0:T(512)(128)(4,1)}, u32[]{:S(2)}) copy-start(pred[4]{0:T(512)(128)(4,1)} %get-tuple-element.6) | copy-start | bytes 16
  361.4 15.0 %copy-start.89 = (pred[4]{0:T(512)(128)(4,1)S(1)}, pred[4]{0:T(512)(128)(4,1)}, u32[]{:S(2)}) copy-start(pred[4]{0:T(512)(128)(4,1)} %get-tuple-element.89) | copy-start | bytes 16
  361.4 5.9 collective-permute-start.2
  364.9 12.2 %copy-start.78 = (pred[4]{0:T(512)(128)(4,1)S(1)}, pred[4]{0:T(512)(128)(4,1)}, u32[]{:S(2)}) copy-start(pred[4]{0:T(512)(128)(4,1)} %get-tuple-element.14) | copy-start | bytes 16
  364.9 12.2 %copy-start.88 = (pred[4]{0:T(512)(128)(4,1)S(1)}, pred[4]{0:T(512)(128)(4,1)}, u32[]{:S(2)}) copy-start(pred[4]{0:T(512)(128)(4,1)} %get-tuple-element.90) | copy-start | bytes 16
  365.8 4.2 collective-permute-start.3
  379.4 3.0 copy-start.10
  414.6 10.3 %copy-start.72 = (s32[4]{0:T(128)S(1)}, s32[4]{0:T(128)}, u32[]{:S(2)}) copy-start(s32[4]{0:T(128)} %copy-done.70) | copy-start | bytes 52
  435.9 65.4 %all-to-all-start.3 = ((bf16[32,2,32768]{2,1,0:T(2,128)(2,1)}), bf16[32,2,32768]{2,1,0:T(2,128)(2,1)}, u32[]{:S(2)}, u32[]{:S(2)}) async-start(bf16[32,2,32768]{2,1,0:T(2,128)(2,1)} %reshape.520), calls=%async_computation.3 | async-start | bytes 8388608 | tf_op jit(solution)/shard_map/all_to_all | solution.py:299
  447.9 229.0 %all-reduce.3.cloned.1.call-start = ((), (), s32[]{:S(2)}) async-start(), calls=%async_computation.4 | async-start | bytes 1048576 | tf_op jit(solution)/shard_map/psum | solution.py:314
  511.4 3.2 copy-start.25
  513.1 4.8 copy-start.27
  513.1 4.8 copy-start.29
  513.1 4.8 copy-start.33
  519.8 1.9 copy-start.53
  521.7 1.9 copy-start.49
  523.5 1.9 copy-start.55
  525.4 1.9 copy-start.57
  530.9 4.2 copy-start.58
  (41 other events, 63.0 us)
Sparse Core Ops, SparseCore 0:
  535.3 141.5 all-reduce.2
where the time goes:
time: 699 us; the launch traced here: 685 us
  waiting for transfers between devices  208 us (30%)
  local copies, waits for them, and re-layouts  205 us (29%)
  matrix products  111 us (16%)
  blocking collectives  63.4 us (9%)
  other arithmetic  42.2 us (6%)
  starting transfers between devices  40.7 us (6%)
  between operations  15.7 us (2%)
    psum x1, waiting for transfers between devices, per_device(): lax.psum((coarse_term, decoder_term), ('dp', 'slab'))  78 us
    psum x1, blocking collectives, per_device(): lax.psum((coarse_term, decoder_term), ('dp', 'slab'))  63.4 us
    reshape x26, local copies, waits for them, and re-layouts, coarse_patch(): window[..., step_x * channels:(step_x + block_edge) * channels]  59.6 us
    all_to_all x1, waiting for transfers between devices, per_device(): lax.all_to_all(outgoing.reshape(slab_count, send_cap, -1), 'slab', split_...  51.6 us
    all_to_all x1, waiting for transfers between devices, per_device(): lax.all_to_all(back_items.reshape(slab_count, send_cap, -1), 'slab', spli...  47.3 us
    all_to_all x1, waiting for transfers between devices, per_device(): lax.all_to_all(outgoing_cot.reshape(slab_count, send_cap, -1), 'slab', sp...  28.8 us
    dot_general x9, matrix products, spread_pooled(): jnp.einsum('bzyp,pq->bzyq', window, band[step_z, step_y], preferred_eleme...  26.4 us
    dot_general x9, matrix products, kernel_term(): jnp.einsum('bzyr,bzyx->rx', window, cotangent, preferred_element_type=jnp...  21.4 us
  transfers between devices with their start and end apart: 9, of which 5 were waited for; matrix products, arithmetic and copies ran while one was open for 11% of the time, Pallas kernels for 0%

commit v1 on v0

v1 whole, which is shorter than its diff:
```python
import jax
import jax.numpy as jnp
from jax import lax
from jax.experimental import pallas as pl
from jax.experimental.pallas import tpu as pltpu
from jax.sharding import PartitionSpec as P

F32 = jnp.float32
BF16 = jnp.bfloat16
VM = pl.BlockSpec(memory_space=pltpu.VMEM)
SM = pl.BlockSpec(memory_space=pltpu.SMEM)
B = 4


def iota(shape, dim):
    return lax.broadcasted_iota(jnp.int32, shape, dim)


def lane_roll(v, shift):
    return pltpu.roll(v, shift % 128, v.ndim - 1)


def group_at(dz, dy):
    if dz == 0:
        return 24 * dy
    if dz == 2:
        return 128 + 24 * dy
    return 72 + 24 * dy if dy < 2 else 128 + 72


def pool_phase(feat_ref, pooled_ref):
    row, col = iota((64, 256), 0), iota((64, 256), 1)
    hit = (row // 8 == col // 32) & (row % 8 == (col % 16) // 2)
    gather = jnp.where(hit, 0.125, 0.0).astype(BF16)
    low = iota((64, 128), 1) < 64
    for b in range(B):
        rows = jnp.dot(gather, feat_ref[b].reshape(256, 1024), preferred_element_type=F32)
        for p in range(4):
            first = rows[:, 256 * p : 256 * p + 128]
            second = rows[:, 256 * p + 128 : 256 * p + 256]
            both = jnp.where(low, first + lane_roll(first, 64), second + lane_roll(second, 64))
            both = both.astype(BF16).astype(F32)
            for z in range(8):
                pooled_ref[z, 8 * b : 8 * b + 8, 128 * p : 128 * p + 128] = both[8 * z : 8 * z + 8]


def coarse_weights(wide_ref, band_ref):
    low = iota((64, 128), 1) < 64
    zero = jnp.zeros((64, 128), F32)
    for k in range(9):
        taps = [wide_ref[3 * k + dx].astype(F32) for dx in range(3)]
        for t in range(2):
            for kx in range(8):
                d0 = kx - 1 - 2 * t
                d1 = d0 - 1
                v0 = taps[d0] if 0 <= d0 < 3 else zero
                v1 = taps[d1] if 0 <= d1 < 3 else zero
                band_ref[k, 64 * kx : 64 * kx + 64, 128 * t : 128 * t + 128] = jnp.where(
                    low, v0, v1
                ).astype(BF16)


def frame_coarse(meta, pooled_ref, sib_ref, frame_ref, zh):
    row = iota((8, 768), 0)

    def masked(cond, v):
        return jnp.where(cond, v, jnp.zeros_like(v))

    def roles(b, col):
        bx, by = meta[b, 0], meta[b, 1]
        found = {}
        for a in range(B):
            ax, ay = meta[a, col], meta[a, col + 1]
            same = (ax >= 0) & (bx >= 0) & ((ax >> 1) == (bx >> 1)) & ((ay >> 1) == (by >> 1))
            for key in ((0, 0), (0, 1), (1, 0), (1, 1)):
                hit = same & ((ax != bx) == bool(key[0])) & ((ay != by) == bool(key[1]))
                found[key] = jnp.where(hit, a, found.get(key, -1))
        return found

    def rows_of(view, who, b):
        xh, yh = meta[b, 0] & 1, meta[b, 1] & 1

        def take(key, lo, hi):
            i = who[key]
            at = pl.multiple_of(jnp.maximum(i, 0) * 8, 8)
            return masked(i >= 0, view(pl.ds(at, 8), slice(lo, hi)))

        def wide(mid, side):
            return jnp.concatenate(
                [
                    masked(xh == 1, take(side, 384, 512)),
                    take(mid, 0, 512),
                    masked(xh == 0, take(side, 0, 128)),
                ],
                axis=1,
            )

        own = wide((0, 0), (1, 0))
        near = wide((0, 1), (1, 1))
        before = jnp.where(row == 0, masked(yh == 1, pltpu.roll(near, 1, 0)), pltpu.roll(own, 1, 0))
        after = jnp.where(row == 7, masked(yh == 0, pltpu.roll(near, 7, 0)), pltpu.roll(own, 7, 0))
        return before, own, after

    own_roles = [roles(b, 0) for b in range(B)]
    sib_roles = [roles(b, 2) for b in range(B)]

    def one_plane(z, unused):
        for q in range(2):
            pair = [
                rows_of(lambda r, c: pooled_ref[z, r, c], own_roles[b], b) for b in (2 * q, 2 * q + 1)
            ]
            for dy in range(3):
                frame_ref[dy, z + 1, 16 * q : 16 * q + 16, :] = jnp.concatenate(
                    [pair[0][dy], pair[1][dy]], axis=0
                ).astype(BF16)
        return unused

    lax.fori_loop(0, 8, one_plane, 0)
    for q in range(2):
        pair = [rows_of(lambda r, c: sib_ref[r, c], sib_roles[b], b) for b in (2 * q, 2 * q + 1)]
        for dy in range(3):
            both = jnp.concatenate([pair[0][dy], pair[1][dy]], axis=0)
            frame_ref[dy, 0, 16 * q : 16 * q + 16, :] = masked(zh == 1, both).astype(BF16)
            frame_ref[dy, 9, 16 * q : 16 * q + 16, :] = masked(zh == 0, both).astype(BF16)


def coarse_conv(frame_ref, band_ref, pre_ref):
    for h in range(2):
        total = None
        for dz in range(3):
            for dy in range(3):
                lhs = frame_ref[dy, dz : dz + 8, :, 256 * h : 256 * h + 512].reshape(256, 512)
                term = jnp.dot(lhs, band_ref[3 * dz + dy], preferred_element_type=F32)
                total = term if total is None else total + term
        pre_ref[:, :, 256 * h : 256 * h + 256] = total.reshape(8, 32, 256)


def mix_phase(meta, feat_ref, pre_ref, up_ref, mixed_ref):
    low = iota((8, 128), 1) < 64

    def one(zc, unused):
        for b in range(B):
            alive = meta[b, 0] >= 0
            for p in range(4):
                v = pre_ref[zc, 8 * b : 8 * b + 8, 128 * p : 128 * p + 128]
                v = jnp.maximum(v, 0.0).astype(BF16).astype(F32)
                turned = lane_roll(v, 64)
                for half in range(2):
                    d = jnp.where(low, v, turned) if half == 0 else jnp.where(low, turned, v)
                    for r in range(2):
                        up_ref[8 * b + 2 * p + half, pl.ds(r, 8, stride=2), :] = d
            for l in range(8):
                u = up_ref[8 * b + l]
                for r in range(2):
                    f = feat_ref[b, 2 * zc + r, :, 128 * l : 128 * l + 128].astype(F32)
                    m = jnp.where(alive, f + u, 0.0)
                    mixed_ref[b, 2 * zc + r, :, 128 * l : 128 * l + 128] = m.astype(BF16)
        return unused

    lax.fori_loop(0, 8, one, 0)


def decoder_bands(wdec_ref, bandt_ref):
    xi = iota((24, 128), 0)
    half = iota((24, 128), 1) // 64
    bandt_ref[...] = jnp.zeros_like(bandt_ref)
    for dz in range(3):
        for dy in range(3):
            taps = [
                jnp.broadcast_to(wdec_ref[9 * dz + 3 * dy + dx : 9 * dz + 3 * dy + dx + 1, :], (24, 128))
                for dx in range(3)
            ]
            at = group_at(dz, dy)
            for l in range(8):
                x = 2 * l + half
                v = jnp.zeros((24, 128), F32)
                for dx in range(3):
                    v = jnp.where(xi == x - dx + 2, taps[dx], v)
                bandt_ref[at : at + 24, 128 * l : 128 * l + 128] = v


def decode_phase(mixed_ref, bandt_ref, tiles_ref, part_ref, up_edge, down_edge):
    lane = iota((16, 128), 1)
    bandt = bandt_ref[...].astype(BF16)
    for b in range(B):
        tiles = lax.dot_general(
            mixed_ref[b].reshape(256, 1024),
            bandt,
            (((1,), (1,)), ((), ())),
            preferred_element_type=F32,
        )
        tiles_ref[...] = tiles.reshape(16, 16, 256)
        up_edge[b] = tiles_ref[15, :, 0:128]
        down_edge[b] = tiles_ref[0, :, 128:256]
        for z in range(16):
            t0, t1 = tiles_ref[z, :, 0:128], tiles_ref[z, :, 128:256]
            v = jnp.where(lane < 48, lane_roll(t0, -72), lane_roll(t1, -24))
            if z > 0:
                v = v + tiles_ref[z - 1, :, 0:128]
            if z < 15:
                v = v + tiles_ref[z + 1, :, 128:256]
            part_ref[b, z] = v


def masked_slot(ref, link):
    v = ref[jnp.maximum(link, 0)]
    return jnp.where(link >= 0, v, jnp.zeros_like(v))


def target_phase(target_ref, wide_ref):
    for y in range(16):
        j, k = y // 8, y % 8
        v = target_ref[:, 128 * j : 128 * j + 128]
        wide_ref[pl.ds(y, 64, stride=16), :] = lane_roll(v, 1 - 16 * k)


def predict_phase(meta, part_ref, below_ref, above_ref, wide_ref, sum_ref, cot_ref, res_ref, out_ref):
    for b in range(B):
        part_ref[b, 0] = part_ref[b, 0] + masked_slot(below_ref, meta[b, 4])
        part_ref[b, 15] = part_ref[b, 15] + masked_slot(above_ref, meta[b, 5])
    row, lane = iota((16, 128), 0), iota((16, 128), 1)
    for b in range(B):
        lo, hi = meta[b, 6], meta[b, 7]

        def along_y(z, unused, b=b, lo=lo, hi=hi):
            own = part_ref[b, z]
            low = part_ref[jnp.maximum(lo, 0), z]
            low = jnp.where(lo >= 0, low, jnp.zeros_like(low))
            high = part_ref[jnp.maximum(hi, 0), z]
            high = jnp.where(hi >= 0, high, jnp.zeros_like(high))
            d0 = jnp.where(row == 0, pltpu.roll(low, 1, 0), pltpu.roll(own, 1, 0))
            d2 = jnp.where(row == 15, pltpu.roll(high, 15, 0), pltpu.roll(own, 15, 0))
            sum_ref[b, z] = d0 + lane_roll(own, -24) + lane_roll(d2, -48)
            return unused

        lax.fori_loop(0, 16, along_y, 0)
    for b in range(B):
        lo, hi = meta[b, 8], meta[b, 9]

        def along_x(z, unused, b=b, lo=lo, hi=hi):
            own = sum_ref[b, z]
            low = sum_ref[jnp.maximum(lo, 0), z]
            high = sum_ref[jnp.maximum(hi, 0), z]
            own = own + jnp.where((lane == 1) & (lo >= 0), lane_roll(low, -16), 0.0)
            own = own + jnp.where((lane == 16) & (hi >= 0), lane_roll(high, 16), 0.0)
            at = pl.multiple_of(256 * b + 16 * z, 16)
            measured = wide_ref[pl.ds(at, 16), :]
            keep = (lane >= 1) & (lane <= 16) & (meta[b, 0] >= 0)
            res = jnp.where(keep, own - measured, 0.0)
            res_ref[pl.ds(at, 16), :] = res
            cot_ref[b, z] = (res * (1.0 / 16384)).astype(BF16).astype(F32)
            return unused

        lax.fori_loop(0, 16, along_x, 0)
    group = iota((64, 128), 1) // 16
    for j in range(2):
        v = jnp.zeros((64, 128), F32)
        for k in range(8):
            got = lane_roll(res_ref[pl.ds(8 * j + k, 64, stride=16), :], 16 * k - 1)
            v = jnp.where(group == k, got, v)
        out_ref[:, 128 * j : 128 * j + 128] = v


def spread_x(lane, own, low, high, lo, hi):
    own = jnp.where(lane == 0, jnp.where(lo >= 0, lane_roll(low, -16), 0.0), own)
    return jnp.where(lane == 17, jnp.where(hi >= 0, lane_roll(high, 16), 0.0), own)


def extend_phase(meta, cot_ref, ext_ref):
    lane = iota((16, 128), 1)
    for b in range(B):
        lo, hi = meta[b, 8], meta[b, 9]

        def along_x(z, unused, b=b, lo=lo, hi=hi):
            low = cot_ref[jnp.maximum(lo, 0), z]
            high = cot_ref[jnp.maximum(hi, 0), z]
            ext_ref[b, z + 1, 8:24, :] = spread_x(lane, cot_ref[b, z], low, high, lo, hi)
            return unused

        lax.fori_loop(0, 16, along_x, 0)
    for b in range(B):
        lo, hi = meta[b, 6], meta[b, 7]
        low = ext_ref[jnp.maximum(lo, 0), 1:17, 23:24, :]
        high = ext_ref[jnp.maximum(hi, 0), 1:17, 8:9, :]
        ext_ref[b, 1:17, 7:8, :] = jnp.where(lo >= 0, low, jnp.zeros_like(low))
        ext_ref[b, 1:17, 24:25, :] = jnp.where(hi >= 0, high, jnp.zeros_like(high))


def adjoint_phase(meta, ext_ref, below_ref, above_ref, taps_ref, cat_ref):
    for b in range(B):
        ext_ref[b, 0] = masked_slot(below_ref, meta[b, 4]).astype(F32)
        ext_ref[b, 17] = masked_slot(above_ref, meta[b, 5]).astype(F32)
    lane = iota((16, 128), 1)
    for b in range(B):

        def gather(z, unused, b=b):
            s0, s1, s2 = (ext_ref[b, z, 9 - dy : 25 - dy, :] for dy in range(3))
            taps_ref[z] = jnp.where(
                lane < 24, s0, jnp.where(lane < 48, lane_roll(s1, 24), lane_roll(s2, 48))
            )
            return unused

        lax.fori_loop(0, 18, gather, 0)

        def place(z, unused, b=b):
            mid = taps_ref[z + 1]
            t0 = jnp.where(lane < 72, taps_ref[z + 2], lane_roll(mid, 72))
            t1 = jnp.where(lane < 72, taps_ref[z], lane_roll(mid, 24))
            cat_ref[b, z] = jnp.concatenate([t0, t1], axis=1).astype(BF16)
            return unused

        lax.fori_loop(0, 16, place, 0)


def decoder_grad(cat_ref, mixed_ref, cross_ref, out_ref):
    cross_ref[...] = lax.dot_general(
        cat_ref[...].reshape(1024, 256),
        mixed_ref[...].reshape(1024, 1024),
        (((0,), (0,)), ((), ())),
        preferred_element_type=F32,
    )
    xi = iota((24, 128), 0)
    half = iota((24, 128), 1) // 64
    for dz in range(3):
        for dy in range(3):
            at = group_at(dz, dy)
            sums = [jnp.zeros((24, 128), F32) for _ in range(3)]
            for l in range(8):
                v = cross_ref[at : at + 24, 128 * l : 128 * l + 128]
                for dx in range(3):
                    sums[dx] = sums[dx] + jnp.where(xi == 2 * l + half - dx + 2, v, 0.0)
            for dx in range(3):
                line = jnp.sum(sums[dx], axis=0, keepdims=True)
                line = line + lane_roll(line, 64)
                tap = 9 * dz + 3 * dy + dx
                out_ref[tap : tap + 1, :] = line


def spread_frame(meta, cot_ref, below_ref, above_ref, tall_ref, full_ref):
    lane = iota((16, 128), 1)
    inner = (lane >= 1) & (lane <= 16)
    for b in range(B):
        for edge, ref, col in ((0, below_ref, 4), (17, above_ref, 5)):
            got = masked_slot(ref, meta[b, col]).astype(F32)[8:24]
            tall_ref[b, edge, 8:24, :] = jnp.where(inner, got, 0.0)
        tall_ref[b, 1:17, 8:24, :] = cot_ref[b]
    for b in range(B):
        lo, hi = meta[b, 6], meta[b, 7]
        low = tall_ref[jnp.maximum(lo, 0), :, 23:24, :]
        high = tall_ref[jnp.maximum(hi, 0), :, 8:9, :]
        tall_ref[b, :, 7:8, :] = jnp.where(lo >= 0, low, jnp.zeros_like(low))
        tall_ref[b, :, 24:25, :] = jnp.where(hi >= 0, high, jnp.zeros_like(high))
    wide = iota((32, 128), 1)
    for b in range(B):
        lo, hi = meta[b, 8], meta[b, 9]

        def along_x(z, unused, b=b, lo=lo, hi=hi):
            low = tall_ref[jnp.maximum(lo, 0), z]
            high = tall_ref[jnp.maximum(hi, 0), z]
            full_ref[b, z] = spread_x(wide, tall_ref[b, z], low, high, lo, hi)
            return unused

        lax.fori_loop(0, 18, along_x, 0)


def spread_gather(full_ref, lhs_ref):
    group = iota((8, 128), 1) // 32

    def planes(z):
        got = []
        for b in range(B):
            v = full_ref[b, z, pl.ds(7, 8, stride=2), :]
            for j in range(1, 4):
                turned = lane_roll(full_ref[b, z, pl.ds(7 + j, 8, stride=2), :], 32 * j)
                v = jnp.where(group == j, turned, v)
            got.append(v)
        return jnp.concatenate(got, axis=0).astype(BF16)

    for z in range(18):
        p = planes(z)
        for i in range(z % 2, 4, 2):
            zc = (z - i) // 2
            if 0 <= zc < 8:
                lhs_ref[zc, :, 128 * i : 128 * i + 128] = p


def spread_weights(wdec_ref, high_ref, low_ref):
    row, col = iota((64, 32), 0), iota((64, 32), 1)

    def pick(k, d):
        return ((k == 2 - d) | (k == 3 - d)).astype(F32)

    sel = pick(row // 16, col // 9) * pick((row // 4) % 4, (col // 3) % 3) * pick(row % 4, col % 3)
    sel = jnp.where(col < 27, sel, 0.0).astype(BF16)
    summed = jnp.dot(sel, wdec_ref[...].astype(BF16), preferred_element_type=F32)
    x = iota((32, 128), 0)
    half = iota((32, 128), 1) // 64
    for ij in range(16):
        taps = [jnp.broadcast_to(summed[4 * ij + k : 4 * ij + k + 1, :], (32, 128)) for k in range(4)]
        for t in range(4):
            v = jnp.zeros((32, 128), F32)
            for k in range(4):
                v = jnp.where(x - 2 * (2 * t + half) == k, taps[k], v)
            hi = v.astype(BF16)
            high_ref[32 * ij : 32 * ij + 32, 128 * t : 128 * t + 128] = hi
            low_ref[32 * ij : 32 * ij + 32, 128 * t : 128 * t + 128] = (v - hi.astype(F32)).astype(BF16)


def dpre_phase(meta, lhs_ref, high_ref, low_ref, pre_ref, dpre_ref):
    lhs = lhs_ref[...].reshape(256, 512)
    up = jnp.dot(lhs, high_ref[...], preferred_element_type=F32)
    up = up + jnp.dot(lhs, low_ref[...], preferred_element_type=F32)
    up = up.astype(BF16).astype(F32).reshape(8, 32, 512)
    for b in range(B):
        mine = up[:, 8 * b : 8 * b + 8]
        keep = (pre_ref[:, 8 * b : 8 * b + 8] > 0) & (meta[b, 0] >= 0)
        dpre_ref[:, 8 * b : 8 * b + 8] = jnp.where(keep, mine, 0.0)


def coarse_grad(frame_ref, dpre_ref, cross_ref, turn_ref, out_ref):
    dpre = dpre_ref[...].reshape(256, 512)
    turned = [dpre[:, 256 * h : 256 * h + 256].T.astype(BF16) for h in range(2)]
    low = iota((64, 128), 1) < 64
    low32 = iota((32, 128), 1) < 64
    pending = []
    for k in range(9):
        dz, dy = k // 3, k % 3
        total = None
        for h in range(2):
            rhs = frame_ref[dy, dz : dz + 8, :, 256 * h : 256 * h + 512].reshape(256, 512)
            term = jnp.dot(turned[h], rhs, preferred_element_type=F32)
            total = term if total is None else total + term
        cross_ref[...] = total
        for dx in range(3):
            sums = [None, None]
            for n in range(4):
                m = n + dx + 1
                v = cross_ref[64 * n : 64 * n + 64, 128 * (m // 2) : 128 * (m // 2) + 128]
                sums[m % 2] = v if sums[m % 2] is None else sums[m % 2] + v
            pending.append((3 * k + dx, sums[0] + lane_roll(sums[1], 64)))
            if len(pending) == 2 or 3 * k + dx == 26:
                first = pending[0][1]
                second = lane_roll(pending[-1][1], 64)
                turn_ref[:, 0:64] = jnp.where(low, first, second).T
                for i, (tap, _) in enumerate(pending):
                    even = turn_ref[pl.ds(64 * i, 32, stride=2), :]
                    odd = turn_ref[pl.ds(64 * i + 1, 32, stride=2), :]
                    out_ref[pl.ds(tap, 32, stride=32), :] = jnp.where(low32, even, lane_roll(odd, 64))
                pending = []


def first_kernel(feat_ref, pooled_ref, plane_ref):
    zh = lax.axis_index("slab") % 2
    pool_phase(feat_ref, pooled_ref)
    plane_ref[...] = pooled_ref[jnp.where(zh == 0, 7, 0)].astype(BF16)


def second_kernel(
    meta, feat_ref, pooled_ref, sib_in, wide_ref, wdec_ref,
    mixed_ref, part_ref, up_edge, down_edge, frame_ref, pre_ref,
    sib_ref, band_ref, up_ref, bandt_ref, tiles_ref,
):
    zh = lax.axis_index("slab") % 2
    coarse_weights(wide_ref, band_ref)
    decoder_bands(wdec_ref, bandt_ref)
    sib_ref[...] = sib_in[...].astype(F32)
    frame_coarse(meta, pooled_ref, sib_ref, frame_ref, zh)
    coarse_conv(frame_ref, band_ref, pre_ref)
    mix_phase(meta, feat_ref, pre_ref, up_ref, mixed_ref)
    decode_phase(mixed_ref, bandt_ref, tiles_ref, part_ref, up_edge, down_edge)


def third_kernel(
    meta, part_in, below_ref, above_ref, target_ref,
    out_ref, cot_ref, low_plane, high_plane, ext_ref,
    part_ref, wide_ref, sum_ref, res_ref,
):
    part_ref[...] = part_in[...]
    target_phase(target_ref, wide_ref)
    predict_phase(meta, part_ref, below_ref, above_ref, wide_ref, sum_ref, cot_ref, res_ref, out_ref)
    extend_phase(meta, cot_ref, ext_ref)
    for b in range(B):
        low_plane[b] = ext_ref[b, 1].astype(BF16)
        high_plane[b] = ext_ref[b, 16].astype(BF16)


def fourth_kernel(
    meta, cot_ref, ext_in, below_ref, above_ref, wdec_ref, mixed_ref, frame_ref, pre_ref,
    dec_ref, coarse_ref,
    ext_ref, taps_ref, cat_ref, dcross_ref, tall_ref, full_ref, lhs_ref, high_ref, low_ref, dpre_ref,
    cross_ref, turn_ref,
):
    ext_ref[...] = ext_in[...]
    adjoint_phase(meta, ext_ref, below_ref, above_ref, taps_ref, cat_ref)
    decoder_grad(cat_ref, mixed_ref, dcross_ref, dec_ref)
    spread_weights(wdec_ref, high_ref, low_ref)
    spread_frame(meta, cot_ref, below_ref, above_ref, tall_ref, full_ref)
    spread_gather(full_ref, lhs_ref)
    dpre_phase(meta, lhs_ref, high_ref, low_ref, pre_ref, dpre_ref)
    coarse_grad(frame_ref, dpre_ref, cross_ref, turn_ref, coarse_ref)


def shape(dims, dtype=F32):
    return jax.ShapeDtypeStruct(dims, dtype)


def call(body, ins, outs, scratch):
    return pl.pallas_call(
        body,
        in_specs=ins,
        out_shape=outs,
        out_specs=[VM] * len(outs),
        scratch_shapes=[pltpu.VMEM(d, t) for d, t in scratch],
        compiler_params=pltpu.CompilerParams(vmem_limit_bytes=48 * 1024 * 1024),
    )


def per_device(features, target, block_coords, neighbours, owners, coarse_weight, decoder_weight):
    feat = features[0, 0]
    coords = block_coords[0, 0]
    count = lax.axis_size("slab")
    sib_coords = lax.ppermute(coords, "slab", [(i, i ^ 1) for i in range(count)])
    meta = jnp.concatenate(
        [coords, sib_coords, neighbours[0, 0], jnp.zeros((B, 6), jnp.int32)], axis=1
    )
    w3 = coarse_weight.reshape(27, 64, 64)
    wide = jnp.concatenate([w3, w3], axis=2)
    wdec = jnp.pad(
        jnp.concatenate([decoder_weight, decoder_weight], axis=1).astype(F32), ((0, 5), (0, 0))
    )
    pooled, plane = call(
        first_kernel, [VM], [shape((8, 32, 512)), shape((32, 512), BF16)], []
    )(feat)
    sib = lax.ppermute(plane, "slab", [(i, i ^ 1) for i in range(count)])
    mixed, part, up_edge, down_edge, frame, pre = call(
        second_kernel,
        [SM] + [VM] * 5,
        [
            shape((4, 16, 16, 1024), BF16),
            shape((4, 16, 16, 128)),
            shape((4, 16, 128)),
            shape((4, 16, 128)),
            shape((3, 10, 32, 768), BF16),
            shape((8, 32, 512)),
        ],
        [
            ((32, 512), F32),
            ((9, 512, 256), BF16),
            ((32, 16, 128), F32),
            ((256, 1024), F32),
            ((16, 16, 256), F32),
        ],
    )(meta, feat, pooled, sib, wide, wdec)
    up = [(i, i + 1) for i in range(count - 1)]
    down = [(j, i) for i, j in up]
    below = lax.ppermute(up_edge, "slab", up)
    above = lax.ppermute(down_edge, "slab", down)
    res, cot, low_plane, high_plane, ext = call(
        third_kernel,
        [SM] + [VM] * 4,
        [
            shape((64, 256)),
            shape((4, 16, 16, 128)),
            shape((4, 32, 128), BF16),
            shape((4, 32, 128), BF16),
            shape((4, 18, 32, 128)),
        ],
        [
            ((4, 16, 16, 128), F32),
            ((1024, 128), F32),
            ((4, 16, 16, 128), F32),
            ((1024, 128), F32),
        ],
    )(meta, part, below, above, target[0, 0].reshape(64, 256))
    cot_below = lax.ppermute(high_plane, "slab", up)
    cot_above = lax.ppermute(low_plane, "slab", down)
    dec, coarse = call(
        fourth_kernel,
        [SM] + [VM] * 8,
        [shape((32, 128)), shape((1024, 128))],
        [
            ((4, 18, 32, 128), F32),
            ((18, 16, 128), F32),
            ((4, 16, 16, 256), BF16),
            ((256, 1024), F32),
            ((4, 18, 32, 128), F32),
            ((4, 18, 32, 128), F32),
            ((8, 32, 512), BF16),
            ((512, 512), BF16),
            ((512, 512), BF16),
            ((8, 32, 512), F32),
            ((256, 512), F32),
            ((128, 128), F32),
        ],
    )(meta, cot, ext, cot_below, cot_above, wdec, mixed, frame, pre)
    mine = lax.psum_scatter(coarse.reshape(32, 32, 128), "slab", scatter_dimension=0, tiled=False)
    mine = lax.psum(mine, "dp")[:27]
    dec = lax.psum(dec[:27, :64], ("dp", "slab"))
    return res.reshape(1, 1, B, 16, 256), mine, dec


def solution(mesh):
    placed = (
        P("dp", "slab", None, None, None, None),
        P("dp", "slab", None, None, None),
        P("dp", "slab", None, None),
        P("dp", "slab", None, None),
        P("dp", "slab", None, None),
        P(),
        P(),
    )
    return jax.shard_map(
        per_device,
        mesh=mesh,
        in_specs=placed,
        out_specs=(P("dp", "slab", None, None, None), P(None, "slab"), P()),
        check_vma=False,
    )
```

time: 699 us -> 182 us (0.26); the launches traced: 685 us -> 182 us
  local copies, waits for them, and re-layouts: 205 us -> 4.22 us
  waiting for transfers between devices: 208 us -> 17.2 us
  matrix products: 111 us -> 0 us
  Pallas kernels: 0 us -> 45.4 us
  other arithmetic: 42.2 us -> 0.4 us
  starting transfers between devices: 40.7 us -> 9.84 us
  blocking collectives: 63.4 us -> 90.5 us
    all_to_all x4 -> x0, waiting for transfers between devices: 128 us -> none  [the longest x1 51.6 us: per_device(): lax.all_to_all(outgoing.reshape(slab_count, send_cap, -1), 'slab', split_...]
    reshape x54 -> x1, local copies, waits for them, and re-layouts: 125 us -> 0.44 us  [per_device(): w3 = coarse_weight.reshape(27, 64, 64)]
    dot_general x62 -> x0, matrix products: 111 us -> none  [the longest x9 26.4 us: spread_pooled(): jnp.einsum('bzyp,pq->bzyq', window, band[step_z, step_y], preferred_eleme...]
    psum x1 -> x0, waiting for transfers between devices: 78 us -> none  [per_device(): lax.psum((coarse_term, decoder_term), ('dp', 'slab'))]
    pallas_call x0 -> x4, Pallas kernels: none -> 45.4 us  [the longest x1 22.1 us: per_device(): call(fourth_kernel, [SM] + [VM] * 8, [shape((32, 128)), shape((1024, 128)...]
    all_to_all x4 -> x0, starting transfers between devices: 33.4 us -> none  [the longest x1 11.9 us: per_device(): lax.all_to_all(outgoing_cot.reshape(slab_count, send_cap, -1), 'slab', sp...]
    psum x1 -> x2, blocking collectives: 63.4 us -> 90.5 us  [the longest x1 72.5 us: per_device(): dec = lax.psum(dec[:27, :64], ('dp', 'slab'))]
    convert_element_type x6 -> x0, local copies, waits for them, and re-layouts: 22.5 us -> none  [the longest x2 11.3 us: per_device(): upsample(upward, half_edge, channels).astype(jnp.float32)]
  transfers between devices with their start and end apart: 9 -> 7, of which waited for: 5 -> 3; matrix products, arithmetic and copies ran while one was open for 11% -> 1% of each run, Pallas kernels for 0% -> 0%
where the time goes in v1:
time: 182 us
  blocking collectives  90.5 us (50%)
  Pallas kernels  45.4 us (25%)
  waiting for transfers between devices  17.2 us (9%)
  between operations  14.2 us (8%)
  starting transfers between devices  9.84 us (5%)
  local copies, waits for them, and re-layouts  4.22 us (2%)
    psum x1, blocking collectives, per_device(): dec = lax.psum(dec[:27, :64], ('dp', 'slab'))  72.5 us
    pallas_call x1, Pallas kernels, per_device(): call(fourth_kernel, [SM] + [VM] * 8, [shape((32, 128)), shape((1024, 128)...  22.1 us
    psum x1, blocking collectives, per_device(): mine = lax.psum(mine, 'dp')[:27]  18 us
    pallas_call x1, Pallas kernels, per_device(): call(third_kernel, [SM] + [VM] * 4, [shape((64, 256)), shape((4, 16, 16,...  16.3 us
    reduce_scatter x1, waiting for transfers between devices, per_device(): lax.psum_scatter(coarse.reshape(32, 32, 128), 'slab', scatter_dimension=0...  12.6 us
    pallas_call x1, Pallas kernels, per_device(): call(second_kernel, [SM] + [VM] * 5, [shape((4, 16, 16, 1024), BF16), sha...  6.43 us
    ppermute x1, starting transfers between devices, per_device(): cot_below = lax.ppermute(high_plane, 'slab', up)  4.52 us
  transfers between devices with their start and end apart: 7, of which 3 were waited for; matrix products, arithmetic and copies ran while one was open for 1% of the time, Pallas kernels for 0%

profile of v1, /device:TPU:0, one launch (start us, length us, event | category | flops | bytes accessed | tf_op | source)
XLA Modules:
  0.0 181.8 jit_solution(17247241068200668414)
XLA Ops:
  7.2 0.0 copy-start.5
  7.2 0.0 reduce-scatter.2.cloned.1.call-start
  7.2 0.8 copy.10
  8.0 0.0 collective-permute-start
  8.0 0.0 copy-start
  8.0 1.6 copy-done
  9.6 0.0 copy-start.4
  9.6 0.0 copy-start.3
  9.6 0.6 shard_map.85
  10.2 0.6 collective-permute-start.1
  10.8 0.1 pad.15.clone
  10.8 0.0 copy-done.4
  10.8 0.1 fusion.3.wdec_ref
  10.9 0.0 copy-done.3
  10.9 0.4 reshape.15
  11.4 0.0 copy-start.2
  11.4 0.2 pad_maximum_fusion.wide_ref
  11.6 0.0 collective-permute-done
  11.7 0.0 copy-done.5
  11.7 0.1 add_add_fusion.meta
  11.7 0.0 collective-permute-done.1.sib_in
  11.7 6.4 %shard_map.86 = (bf16[4,16,16,1024]{3,2,1,0:T(8,128)(2,1)S(1)}, f32[4,16,16,128]{3,2,1,0:T(8,128)S(1)}, f32[4,16,128]{2,1,0:T(8,128)S(1)}, f32[4,16,128]{2,1,0:T...) custom-call(s32[4,16]{1,0:T(4,128)S(1)} %add_add_fusion.meta, ...), custom_call_target="tpu_custom_call" | custom-call | tf_op jit(solution)/shard_map/pallas_call | solution.py:535
  18.2 0.0 copy-start.1
  18.2 1.3 copy-done.1
  19.5 2.1 %collective-permute-start.2 = (f32[4,16,128]{2,1,0:T(8,128)S(1)}, f32[4,16,128]{2,1,0:T(8,128)S(1)}, u32[]{:S(2)}, u32[]{:S(2)}) collective-permute-start(f32[4,16,128]{2,1,0:T(8,128)S(1)} %get-tuple-element.21), channel_id=1, source_target_pairs={{0,1},{1,2},{2,3},{3,4},{4,5},{5,6},{6,7},{7,8},{8,9},{9,10},{10,1... | collective-permute-start | bytes 98312 | tf_op jit(solution)/shard_map/ppermute | solution.py:556
  21.6 1.3 collective-permute-start.3
  22.9 0.0 collective-permute-done.2.below_ref
  23.0 2.8 %collective-permute-done.3.above_ref = f32[4,16,128]{2,1,0:T(8,128)S(1)} collective-permute-done((f32[4,16,128]{2,1,0:T(8,128)S(1)}, f32[4,16,128]{2,1,0:T(8,128)S(1)}, u32[]{:S(2)}, u32[]{:S(2)}) %collective-permute-start.3) | collective-permute-done | bytes 32800 | tf_op jit(solution)/shard_map/ppermute | solution.py:557
  25.8 0.0 copy-done.2
  25.8 16.3 %shard_map.87 = (f32[64,256]{1,0:T(8,128)}, f32[4,16,16,128]{3,2,1,0:T(8,128)S(1)}, bf16[4,32,128]{2,1,0:T(8,128)(2,1)S(1)}, bf16[4,32,128]{2,1,0:T(8,128)(2,1)S(1)}, f32[4,18,32,128]{3,2,1,0:T(8,128)S(1)}) custom-call(s32[4,16]{1,0:T(4,128)S(1)} %add_add_fusion.meta, f32[4,16,16,128]{3,2,1,0:T(8,128)S(1)} %get-tuple-element.20.part_in, ...), custom_call_target="tpu_custom_call" | custom-call | tf_op jit(solution)/shard_map/pallas_call | solution.py:558
  42.1 4.5 %collective-permute-start.4 = (bf16[4,32,128]{2,1,0:T(8,128)(2,1)S(1)}, bf16[4,32,128]{2,1,0:T(8,128)(2,1)S(1)}, u32[]{:S(2)}, u32[]{:S(2)}) collective-permute-start(bf16[4,32,128]{2,1,0:T(8,128)(2,1)S(1)} %get-tuple-element.26), channel_id=1, source_target_pairs={{0,1},{1,2},{2,3},{3,4},{4,5},{5,6},{6,7},{7,8},{8,9},{9,10},{10,1... | collective-permute-start | bytes 98312 | tf_op jit(solution)/shard_map/ppermute | solution.py:575
  46.6 1.3 collective-permute-start.5
  47.9 0.0 collective-permute-done.4.below_ref
  47.9 1.8 collective-permute-done.5.above_ref
  49.7 22.1 %shard_map.88 = (f32[32,128]{1,0:T(8,128)S(1)}, f32[1024,128]{1,0:T(8,128)}) custom-call(s32[4,16]{1,0:T(4,128)S(1)} %add_add_fusion.meta, f32[4,16,16,128]{3,2,1,0:T(8,128)S(1)} %get-tuple-element.24.cot_ref, f32[4,18,32,128]{3,2,1,0:T(8,128)S(1)} %get-tuple-element.25.ext_in, bf16[4,32,128]{2,1,0:T(8,128)(2,1)S(1)} %collective-permute-done.4.below_ref, ...), custom_call_target="tpu_custom_call" | custom-call | tf_op jit(solution)/shard_map/pallas_call | solution.py:577
  71.8 0.0 reduce-scatter.2.cloned.1.call-update
  71.8 72.5 %psum.15 = f32[27,64]{1,0:T(8,128)} all-reduce(f32[27,64]{1,0:T(8,128)S(1)} %bitcast.12), channel_id=1, replica_groups=mesh['dp'=4,'slab'=32] {'dp','slab'}, use_global_device_ids=true, to_apply=%region_2.3 | all-reduce | flops 1728 | bytes 13824 | tf_op jit(solution)/shard_map/psum | solution.py:598
  144.3 12.6 %reduce-scatter.2.cloned.1.call-done = f32[1,32,128]{2,1,0:T(8,128)} async-done(((f32[32,32,128]{2,1,0:T(8,128)}), f32[1,32,128]{2,1,0:T(8,128)}) %reduce-scatter.2.cloned.1.call-update) | async-done | bytes 16400 | tf_op jit(solution)/shard_map/reduce_scatter | solution.py:596
  156.9 18.0 %psum.14 = f32[32,128]{1,0:T(8,128)} all-reduce(f32[32,128]{1,0:T(8,128)} %bitcast.13), channel_id=1, replica_groups=mesh['dp'=4,'slab'=32] {'dp'}, use_global_device_ids=true, to_apply=%region_1.2 | all-reduce | flops 4096 | bytes 32768 | tf_op jit(solution)/shard_map/psum | solution.py:597
  (1 shorter events, 0.0 us)
Async XLA Ops:
  7.2 4.5 %copy-start.5 = (s32[1,1,4,6]{3,2,1,0:T(4,128)S(1)}, s32[1,1,4,6]{3,2,1,0:T(4,128)}, u32[]{:S(2)}) copy-start(s32[1,1,4,6]{3,2,1,0:T(4,128)} %param.10) | copy-start | bytes 292
  7.2 149.7 %reduce-scatter.2.cloned.1.call-start = ((), (), s32[]{:S(2)}) async-start(), calls=%async_computation.1 | async-start | bytes 540672 | tf_op jit(solution)/shard_map/reduce_scatter | solution.py:596
  8.0 3.7 %collective-permute-start = (s32[4,2]{1,0:T(4,128)S(1)}, s32[4,2]{1,0:T(4,128)S(1)}, u32[]{:S(2)}, u32[]{:S(2)}) collective-permute-start(s32[4,2]{1,0:T(4,128)S(1)} %copy.10), channel_id=1, source_target_pairs={{0,1},{1,0},{2,3},{3,2},{4,5},{5,4},{6,7},{7,6},{8,9},{9,8},{10,11... | collective-permute-start | bytes 104 | tf_op jit(solution)/shard_map/ppermute | solution.py:522
  8.0 1.6 copy-start
  9.6 1.3 copy-start.4
  9.6 1.3 copy-start.3
  10.2 1.6 collective-permute-start.1
  11.4 14.4 %copy-start.2 = (f32[1,1,4,16,256]{4,3,2,1,0:T(8,128)S(1)}, f32[1,1,4,16,256]{4,3,2,1,0:T(8,128)}, u32[]{:S(2)}) copy-start(f32[1,1,4,16,256]{4,3,2,1,0:T(8,128)} %param.8) | copy-start | bytes 196612
  18.2 1.3 copy-start.1
  19.5 3.4 %collective-permute-start.2 = (f32[4,16,128]{2,1,0:T(8,128)S(1)}, f32[4,16,128]{2,1,0:T(8,128)S(1)}, u32[]{:S(2)}, u32[]{:S(2)}) collective-permute-start(f32[4,16,128]{2,1,0:T(8,128)S(1)} %get-tuple-element.21), channel_id=1, source_target_pairs={{0,1},{1,2},{2,3},{3,4},{4,5},{5,6},{6,7},{7,8},{8,9},{9,10},{10,1... | collective-permute-start | bytes 98312 | tf_op jit(solution)/shard_map/ppermute | solution.py:556
  21.6 4.2 %collective-permute-start.3 = (f32[4,16,128]{2,1,0:T(8,128)S(1)}, f32[4,16,128]{2,1,0:T(8,128)S(1)}, u32[]{:S(2)}, u32[]{:S(2)}) collective-permute-start(f32[4,16,128]{2,1,0:T(8,128)S(1)} %get-tuple-element.22), channel_id=1, source_target_pairs={{1,0},{2,1},{3,2},{4,3},{5,4},{6,5},{7,6},{8,7},{9,8},{10,9},{11,1... | collective-permute-start | bytes 98312 | tf_op jit(solution)/shard_map/ppermute | solution.py:557
  42.1 5.8 %collective-permute-start.4 = (bf16[4,32,128]{2,1,0:T(8,128)(2,1)S(1)}, bf16[4,32,128]{2,1,0:T(8,128)(2,1)S(1)}, u32[]{:S(2)}, u32[]{:S(2)}) collective-permute-start(bf16[4,32,128]{2,1,0:T(8,128)(2,1)S(1)} %get-tuple-element.26), channel_id=1, source_target_pairs={{0,1},{1,2},{2,3},{3,4},{4,5},{5,6},{6,7},{7,8},{8,9},{9,10},{10,1... | collective-permute-start | bytes 98312 | tf_op jit(solution)/shard_map/ppermute | solution.py:575
  46.6 3.1 %collective-permute-start.5 = (bf16[4,32,128]{2,1,0:T(8,128)(2,1)S(1)}, bf16[4,32,128]{2,1,0:T(8,128)(2,1)S(1)}, u32[]{:S(2)}, u32[]{:S(2)}) collective-permute-start(bf16[4,32,128]{2,1,0:T(8,128)(2,1)S(1)} %get-tuple-element.27), channel_id=1, source_target_pairs={{1,0},{2,1},{3,2},{4,3},{5,4},{6,5},{7,6},{8,7},{9,8},{10,9},{11,1... | collective-permute-start | bytes 98312 | tf_op jit(solution)/shard_map/ppermute | solution.py:576
Sparse Core Ops, SparseCore 0:
  71.9 84.9 reduce-scatter.1

commit v2 on v1

--- a/solution.py
+++ b/solution.py
@@ -14,6 +14,18 @@
 
 def iota(shape, dim):
     return lax.broadcasted_iota(jnp.int32, shape, dim)
+
+
+def repeat(count, body, step):
+    def some(i, unused):
+        for k in range(step):
+            body(i * step + k)
+        return unused
+
+    if step == count:
+        some(0, 0)
+    else:
+        lax.fori_loop(0, count // step, some, 0)
 
 
 def lane_roll(v, shift):
@@ -104,7 +116,7 @@
     own_roles = [roles(b, 0) for b in range(B)]
     sib_roles = [roles(b, 2) for b in range(B)]
 
-    def one_plane(z, unused):
+    def one_plane(z):
         for q in range(2):
             pair = [
                 rows_of(lambda r, c: pooled_ref[z, r, c], own_roles[b], b) for b in (2 * q, 2 * q + 1)
@@ -113,9 +125,8 @@
                 frame_ref[dy, z + 1, 16 * q : 16 * q + 16, :] = jnp.concatenate(
                     [pair[0][dy], pair[1][dy]], axis=0
                 ).astype(BF16)
-        return unused
-
-    lax.fori_loop(0, 8, one_plane, 0)
+
+    repeat(8, one_plane, 2)
     for q in range(2):
         pair = [rows_of(lambda r, c: sib_ref[r, c], sib_roles[b], b) for b in (2 * q, 2 * q + 1)]
         for dy in range(3):
@@ -138,7 +149,7 @@
 def mix_phase(meta, feat_ref, pre_ref, up_ref, mixed_ref):
     low = iota((8, 128), 1) < 64
 
-    def one(zc, unused):
+    def one(zc):
         for b in range(B):
             alive = meta[b, 0] >= 0
             for p in range(4):
@@ -155,9 +166,8 @@
                     f = feat_ref[b, 2 * zc + r, :, 128 * l : 128 * l + 128].astype(F32)
                     m = jnp.where(alive, f + u, 0.0)
                     mixed_ref[b, 2 * zc + r, :, 128 * l : 128 * l + 128] = m.astype(BF16)
-        return unused
-
-    lax.fori_loop(0, 8, one, 0)
+
+    repeat(8, one, 1)
 
 
 def decoder_bands(wdec_ref, bandt_ref):
@@ -222,7 +232,7 @@
     for b in range(B):
         lo, hi = meta[b, 6], meta[b, 7]
 
-        def along_y(z, unused, b=b, lo=lo, hi=hi):
+        def along_y(z, b=b, lo=lo, hi=hi):
             own = part_ref[b, z]
             low = part_ref[jnp.maximum(lo, 0), z]
             low = jnp.where(lo >= 0, low, jnp.zeros_like(low))
@@ -231,13 +241,12 @@
             d0 = jnp.where(row == 0, pltpu.roll(low, 1, 0), pltpu.roll(own, 1, 0))
             d2 = jnp.where(row == 15, pltpu.roll(high, 15, 0), pltpu.roll(own, 15, 0))
             sum_ref[b, z] = d0 + lane_roll(own, -24) + lane_roll(d2, -48)
-            return unused
-
-        lax.fori_loop(0, 16, along_y, 0)
+
+        repeat(16, along_y, 8)
     for b in range(B):
         lo, hi = meta[b, 8], meta[b, 9]
 
-        def along_x(z, unused, b=b, lo=lo, hi=hi):
+        def along_x(z, b=b, lo=lo, hi=hi):
             own = sum_ref[b, z]
             low = sum_ref[jnp.maximum(lo, 0), z]
             high = sum_ref[jnp.maximum(hi, 0), z]
@@ -249,9 +258,8 @@
             res = jnp.where(keep, own - measured, 0.0)
             res_ref[pl.ds(at, 16), :] = res
             cot_ref[b, z] = (res * (1.0 / 16384)).astype(BF16).astype(F32)
-            return unused
-
-        lax.fori_loop(0, 16, along_x, 0)
+
+        repeat(16, along_x, 8)
     group = iota((64, 128), 1) // 16
     for j in range(2):
         v = jnp.zeros((64, 128), F32)
@@ -271,13 +279,12 @@
     for b in range(B):
         lo, hi = meta[b, 8], meta[b, 9]
 
-        def along_x(z, unused, b=b, lo=lo, hi=hi):
+        def along_x(z, b=b, lo=lo, hi=hi):
             low = cot_ref[jnp.maximum(lo, 0), z]
             high = cot_ref[jnp.maximum(hi, 0), z]
             ext_ref[b, z + 1, 8:24, :] = spread_x(lane, cot_ref[b, z], low, high, lo, hi)
-            return unused
-
-        lax.fori_loop(0, 16, along_x, 0)
+
+        repeat(16, along_x, 8)
     for b in range(B):
         lo, hi = meta[b, 6], meta[b, 7]
         low = ext_ref[jnp.maximum(lo, 0), 1:17, 23:24, :]
@@ -293,23 +300,21 @@
     lane = iota((16, 128), 1)
     for b in range(B):
 
-        def gather(z, unused, b=b):
+        def gather(z, b=b):
             s0, s1, s2 = (ext_ref[b, z, 9 - dy : 25 - dy, :] for dy in range(3))
             taps_ref[z] = jnp.where(
                 lane < 24, s0, jnp.where(lane < 48, lane_roll(s1, 24), lane_roll(s2, 48))
             )
-            return unused
-
-        lax.fori_loop(0, 18, gather, 0)
-
-        def place(z, unused, b=b):
+
+        repeat(18, gather, 9)
+
+        def place(z, b=b):
             mid = taps_ref[z + 1]
             t0 = jnp.where(lane < 72, taps_ref[z + 2], lane_roll(mid, 72))
             t1 = jnp.where(lane < 72, taps_ref[z], lane_roll(mid, 24))
             cat_ref[b, z] = jnp.concatenate([t0, t1], axis=1).astype(BF16)
-            return unused
-
-        lax.fori_loop(0, 16, place, 0)
+
+        repeat(16, place, 8)
 
 
 def decoder_grad(cat_ref, mixed_ref, cross_ref, out_ref):
@@ -354,13 +359,12 @@
     for b in range(B):
         lo, hi = meta[b, 8], meta[b, 9]
 
-        def along_x(z, unused, b=b, lo=lo, hi=hi):
+        def along_x(z, b=b, lo=lo, hi=hi):
             low = tall_ref[jnp.maximum(lo, 0), z]
             high = tall_ref[jnp.maximum(hi, 0), z]
             full_ref[b, z] = spread_x(wide, tall_ref[b, z], low, high, lo, hi)
-            return unused
-
-        lax.fori_loop(0, 18, along_x, 0)
+
+        repeat(18, along_x, 9)
 
 
 def spread_gather(full_ref, lhs_ref):
@@ -445,7 +449,7 @@
                 for i, (tap, _) in enumerate(pending):
                     even = turn_ref[pl.ds(64 * i, 32, stride=2), :]
                     odd = turn_ref[pl.ds(64 * i + 1, 32, stride=2), :]
-                    out_ref[pl.ds(tap, 32, stride=32), :] = jnp.where(low32, even, lane_roll(odd, 64))
+                    out_ref[pl.ds(tap, 32, stride=48), :] = jnp.where(low32, even, lane_roll(odd, 64))
                 pending = []
 
 
@@ -486,18 +490,128 @@
 
 def fourth_kernel(
     meta, cot_ref, ext_in, below_ref, above_ref, wdec_ref, mixed_ref, frame_ref, pre_ref,
-    dec_ref, coarse_ref,
-    ext_ref, taps_ref, cat_ref, dcross_ref, tall_ref, full_ref, lhs_ref, high_ref, low_ref, dpre_ref,
+    coarse_ref,
+    dec_ref, ext_ref, taps_ref, cat_ref, dcross_ref, tall_ref, full_ref, lhs_ref, high_ref, low_ref, dpre_ref,
     cross_ref, turn_ref,
 ):
     ext_ref[...] = ext_in[...]
     adjoint_phase(meta, ext_ref, below_ref, above_ref, taps_ref, cat_ref)
     decoder_grad(cat_ref, mixed_ref, dcross_ref, dec_ref)
+    even = dec_ref[pl.ds(0, 16, stride=2), :]
+    odd = dec_ref[pl.ds(1, 16, stride=2), :]
+    both = jnp.where(iota((16, 128), 1) < 64, even, odd)
+    for j in range(32):
+        coarse_ref[48 * j + 32 : 48 * j + 48, :] = both
     spread_weights(wdec_ref, high_ref, low_ref)
     spread_frame(meta, cot_ref, below_ref, above_ref, tall_ref, full_ref)
     spread_gather(full_ref, lhs_ref)
     dpre_phase(meta, lhs_ref, high_ref, low_ref, pre_ref, dpre_ref)
     coarse_grad(frame_ref, dpre_ref, cross_ref, turn_ref, coarse_ref)
+
+
+def reduce_kernel(
+    local_ref, coarse_ref, dec_ref,
+    sib_ref, half_ref, chips_ref, parts_ref, pair_sems, chip_sends, chip_recvs, dp_sends, dp_recvs,
+):
+    slab, dp = lax.axis_index("slab"), lax.axis_index("dp")
+    core, chip = slab % 2, slab // 2
+    chips, copies = chips_ref.shape[0], parts_ref.shape[0]
+    sibling = {"slab": slab + 1 - 2 * core}
+    barrier = pltpu.get_barrier_semaphore()
+
+    def greet(device):
+        pl.semaphore_signal(barrier, inc=1, device_id=device, device_id_type=pl.DeviceIdType.MESH)
+
+    def peer(r):
+        return lax.rem(chip + r, chips)
+
+    def twin(r):
+        return lax.rem(dp + r, copies)
+
+    greet(sibling)
+    for r in range(1, chips):
+        greet({"slab": 2 * peer(r) + core})
+    for r in range(1, copies):
+        greet({"dp": twin(r)})
+    pl.semaphore_wait(barrier, chips + copies - 1)
+
+    swap = pltpu.make_async_remote_copy(
+        src_ref=local_ref.at[:, 1 - core],
+        dst_ref=sib_ref,
+        send_sem=pair_sems.at[0],
+        recv_sem=pair_sems.at[1],
+        device_id=sibling,
+        device_id_type=pl.DeviceIdType.MESH,
+    )
+    swap.start()
+    swap.wait()
+    half_ref[...] = local_ref[:, core] + sib_ref[...]
+
+    def to_chip(r):
+        return pltpu.make_async_remote_copy(
+            src_ref=half_ref.at[peer(r)],
+            dst_ref=chips_ref.at[chip],
+            send_sem=chip_sends.at[r],
+            recv_sem=chip_recvs.at[chip],
+            device_id={"slab": 2 * peer(r) + core},
+            device_id_type=pl.DeviceIdType.MESH,
+        )
+
+    def from_chip(r):
+        return pltpu.make_async_remote_copy(
+            src_ref=half_ref.at[chip],
+            dst_ref=chips_ref.at[peer(r)],
+            send_sem=chip_sends.at[r],
+            recv_sem=chip_recvs.at[peer(r)],
+            device_id={"slab": 2 * peer(r) + core},
+            device_id_type=pl.DeviceIdType.MESH,
+        )
+
+    for r in range(1, chips):
+        to_chip(r).start()
+    chips_ref[chip] = half_ref[chip]
+    for r in range(1, chips):
+        from_chip(r).wait_recv()
+    total = chips_ref[0]
+    for k in range(1, chips):
+        total = total + chips_ref[k]
+    parts_ref[dp] = total
+
+    def to_twin(r):
+        return pltpu.make_async_remote_copy(
+            src_ref=parts_ref.at[dp],
+            dst_ref=parts_ref.at[dp],
+            send_sem=dp_sends.at[r],
+            recv_sem=dp_recvs.at[dp],
+            device_id={"dp": twin(r)},
+            device_id_type=pl.DeviceIdType.MESH,
+        )
+
+    def from_twin(r):
+        return pltpu.make_async_remote_copy(
+            src_ref=parts_ref.at[dp],
+            dst_ref=parts_ref.at[twin(r)],
+            send_sem=dp_sends.at[r],
+            recv_sem=dp_recvs.at[twin(r)],
+            device_id={"dp": twin(r)},
+            device_id_type=pl.DeviceIdType.MESH,
+        )
+
+    for r in range(1, copies):
+        to_twin(r).start()
+    for r in range(1, copies):
+        from_twin(r).wait_recv()
+    total = parts_ref[0]
+    for k in range(1, copies):
+        total = total + parts_ref[k]
+    coarse_ref[...] = total[0:27]
+    for tap in range(27):
+        line = total[32 + tap // 2 : 33 + tap // 2]
+        dec_ref[tap : tap + 1, :] = line[:, 64 * (tap % 2) : 64 * (tap % 2) + 64]
+    for r in range(1, chips):
+        to_chip(r).wait_send()
+    for r in range(1, copies):
+        to_twin(r).wait_send()
 
 
 def shape(dims, dtype=F32):
@@ -574,11 +688,12 @@
     )(meta, part, below, above, target[0, 0].reshape(64, 256))
     cot_below = lax.ppermute(high_plane, "slab", up)
     cot_above = lax.ppermute(low_plane, "slab", down)
-    dec, coarse = call(
+    (coarse,) = call(
         fourth_kernel,
         [SM] + [VM] * 8,
-        [shape((32, 128)), shape((1024, 128))],
+        [shape((1536, 128))],
         [
+            ((32, 128), F32),
             ((4, 18, 32, 128), F32),
             ((18, 16, 128), F32),
             ((4, 16, 16, 256), BF16),
@@ -593,9 +708,27 @@
             ((128, 128), F32),
         ],
     )(meta, cot, ext, cot_below, cot_above, wdec, mixed, frame, pre)
-    mine = lax.psum_scatter(coarse.reshape(32, 32, 128), "slab", scatter_dimension=0, tiled=False)
-    mine = lax.psum(mine, "dp")[:27]
-    dec = lax.psum(dec[:27, :64], ("dp", "slab"))
+    chips, copies = count // 2, lax.axis_size("dp")
+    mine, dec = pl.pallas_call(
+        reduce_kernel,
+        in_specs=[VM],
+        out_shape=[shape((27, 128)), shape((27, 64))],
+        out_specs=[VM, VM],
+        scratch_shapes=[
+            pltpu.VMEM((chips, 48, 128), F32),
+            pltpu.VMEM((chips, 48, 128), F32),
+            pltpu.VMEM((chips, 48, 128), F32),
+            pltpu.VMEM((copies, 48, 128), F32),
+            pltpu.SemaphoreType.DMA((2,)),
+            pltpu.SemaphoreType.DMA((chips,)),
+            pltpu.SemaphoreType.DMA((chips,)),
+            pltpu.SemaphoreType.DMA((copies,)),
+            pltpu.SemaphoreType.DMA((copies,)),
+        ],
+        compiler_params=pltpu.CompilerParams(
+            collective_id=0, has_side_effects=True, vmem_limit_bytes=48 * 1024 * 1024
+        ),
+    )(coarse.reshape(chips, 2, 48, 128))
     return res.reshape(1, 1, B, 16, 256), mine, dec
 
 

time: 182 us -> 66.8 us (0.37)
  blocking collectives: 90.5 us -> 0 us
  between operations: 14.2 us -> 0.77 us
  waiting for transfers between devices: 17.2 us -> 4.65 us
    psum x2 -> x0, blocking collectives: 90.5 us -> none  [the longest x1 72.5 us: per_device(): dec = lax.psum(dec[:27, :64], ('dp', 'slab'))]
    reduce_scatter x1 -> x0, waiting for transfers between devices: 12.6 us -> none  [per_device(): lax.psum_scatter(coarse.reshape(32, 32, 128), 'slab', scatter_dimension=0...]
    pallas_call x1 -> x2, Pallas kernels: 22.1 us -> 34.3 us  [the longest x1 25.8 us: per_device(): pl.pallas_call(reduce_kernel, in_specs=[VM], out_shape=[shape((27, 128)),...]
    pallas_call x1, Pallas kernels: 16.3 us -> 4.27 us  [per_device(): call(third_kernel, [SM] + [VM] * 4, [shape((64, 256)), shape((4, 16, 16,...]
    unnamed x12 -> x14, local copies, waits for them, and re-layouts: 2.94 us -> 4.15 us
  transfers between devices with their start and end apart: 7 -> 6, of which waited for: 3 -> 2; matrix products, arithmetic and copies ran while one was open for 1% -> 1% of each run, Pallas kernels for 0% -> 1%
where the time goes in v2:
time: 66.8 us; the launch traced here: 66.5 us
  Pallas kernels  45.4 us (68%)
  starting transfers between devices  9.8 us (15%)
  local copies, waits for them, and re-layouts  5.44 us (8%)
  waiting for transfers between devices  4.65 us (7%)
  between operations  0.77 us (1%)
    pallas_call x1, Pallas kernels, per_device(): pl.pallas_call(reduce_kernel, in_specs=[VM], out_shape=[shape((27, 128)),...  25.8 us
    pallas_call x1, Pallas kernels, per_device(): call(fourth_kernel, [SM] + [VM] * 8, [shape((1536, 128))], [((32, 128), F...  8.46 us
    pallas_call x1, Pallas kernels, per_device(): call(second_kernel, [SM] + [VM] * 5, [shape((4, 16, 16, 1024), BF16), sha...  6.24 us
    ppermute x1, starting transfers between devices, per_device(): cot_below = lax.ppermute(high_plane, 'slab', up)  4.52 us
    pallas_call x1, Pallas kernels, per_device(): call(third_kernel, [SM] + [VM] * 4, [shape((64, 256)), shape((4, 16, 16,...  4.27 us
    unnamed x14, local copies, waits for them, and re-layouts  4.15 us
    ppermute x1, waiting for transfers between devices, per_device(): above = lax.ppermute(down_edge, 'slab', down)  2.85 us
    ppermute x1, starting transfers between devices, per_device(): below = lax.ppermute(up_edge, 'slab', up)  2.12 us
  transfers between devices with their start and end apart: 6, of which 2 were waited for; matrix products, arithmetic and copies ran while one was open for 1% of the time, Pallas kernels for 1%

profile of v2, /device:TPU:0, one launch (start us, length us, event | category | flops | bytes accessed | tf_op | source)
XLA Modules:
  0.0 66.5 jit_solution(15318242327783243790)
XLA Ops:
  0.6 0.0 copy-start.5
  0.6 0.8 %copy.10 = s32[4,2]{1,0:T(4,128)S(1)} copy(s32[4,2]{0,1:T(2,128)} %bitcast.11) | data formatting | bytes 64 | tf_op jit(solution)/shard_map/squeeze | solution.py:634
  1.4 0.0 collective-permute-start
  1.4 0.0 copy-start
  1.4 1.6 %copy-done = bf16[1,1,4,16,16,1024]{5,4,3,2,1,0:T(8,128)(2,1)S(1)} copy-done((bf16[1,1,4,16,16,1024]{5,4,3,2,1,0:T(8,128)(2,1)S(1)}, bf16[1,1,4,16,16,1024]{5,4,3,2,1,0:T(8,128)(2,1)}, u32[]{:S(2)}) %copy-start) | copy-done | bytes 2097176
  3.0 0.0 copy-start.4
  3.0 0.0 copy-start.3
  3.0 0.6 shard_map.85
  3.6 0.6 collective-permute-start.1
  4.2 0.1 pad.15.clone
  4.3 0.0 copy-done.4
  4.3 0.1 fusion.3.wdec_ref
  4.3 0.0 copy-done.3
  4.3 0.4 reshape.15
  4.8 0.0 copy-start.2
  4.8 0.2 pad_maximum_fusion.wide_ref
  5.1 0.0 collective-permute-done
  5.1 0.0 copy-done.5
  5.1 0.1 add_add_fusion.meta
  5.2 0.0 collective-permute-done.1.sib_in
  5.2 6.2 %shard_map.86 = (bf16[4,16,16,1024]{3,2,1,0:T(8,128)(2,1)S(1)}, f32[4,16,16,128]{3,2,1,0:T(8,128)S(1)}, f32[4,16,128]{2,1,0:T(8,128)S(1)}, f32[4,16,128]{2,1,0:T...) custom-call(s32[4,16]{1,0:T(4,128)S(1)} %add_add_fusion.meta, ...), custom_call_target="tpu_custom_call" | custom-call | tf_op jit(solution)/shard_map/pallas_call | solution.py:649
  11.4 0.0 copy-start.1
  11.4 1.3 %copy-done.1 = bf16[4,16,16,1024]{3,2,1,0:T(8,128)(2,1)} copy-done((bf16[4,16,16,1024]{3,2,1,0:T(8,128)(2,1)}, bf16[4,16,16,1024]{3,2,1,0:T(8,128)(2,1)S(1)}, u32[]{:S(2)}) %copy-start.1) | copy-done | bytes 2097176
  12.8 2.1 %collective-permute-start.2 = (f32[4,16,128]{2,1,0:T(8,128)S(1)}, f32[4,16,128]{2,1,0:T(8,128)S(1)}, u32[]{:S(2)}, u32[]{:S(2)}) collective-permute-start(f32[4,16,128]{2,1,0:T(8,128)S(1)} %get-tuple-element.21), channel_id=1, source_target_pairs={{0,1},{1,2},{2,3},{3,4},{4,5},{5,6},{6,7},{7,8},{8,9},{9,10},{10,1... | collective-permute-start | bytes 98312 | tf_op jit(solution)/shard_map/ppermute | solution.py:670
  14.9 1.3 %collective-permute-start.3 = (f32[4,16,128]{2,1,0:T(8,128)S(1)}, f32[4,16,128]{2,1,0:T(8,128)S(1)}, u32[]{:S(2)}, u32[]{:S(2)}) collective-permute-start(f32[4,16,128]{2,1,0:T(8,128)S(1)} %get-tuple-element.22), channel_id=1, source_target_pairs={{1,0},{2,1},{3,2},{4,3},{5,4},{6,5},{7,6},{8,7},{9,8},{10,9},{11,1... | collective-permute-start | bytes 98312 | tf_op jit(solution)/shard_map/ppermute | solution.py:671
  16.2 0.0 collective-permute-done.2.below_ref
  16.2 2.8 %collective-permute-done.3.above_ref = f32[4,16,128]{2,1,0:T(8,128)S(1)} collective-permute-done((f32[4,16,128]{2,1,0:T(8,128)S(1)}, f32[4,16,128]{2,1,0:T(8,128)S(1)}, u32[]{:S(2)}, u32[]{:S(2)}) %collective-permute-start.3) | collective-permute-done | bytes 32800 | tf_op jit(solution)/shard_map/ppermute | solution.py:671
  19.0 0.0 copy-done.2
  19.0 4.3 %shard_map.87 = (f32[64,256]{1,0:T(8,128)}, f32[4,16,16,128]{3,2,1,0:T(8,128)S(1)}, bf16[4,32,128]{2,1,0:T(8,128)(2,1)S(1)}, bf16[4,32,128]{2,1,0:T(8,128)(2,1)S(1)}, f32[4,18,32,128]{3,2,1,0:T(8,128)S(1)}) custom-call(s32[4,16]{1,0:T(4,128)S(1)} %add_add_fusion.meta, f32[4,16,16,128]{3,2,1,0:T(8,128)S(1)} %get-tuple-element.20.part_in, ...), custom_call_target="tpu_custom_call" | custom-call | tf_op jit(solution)/shard_map/pallas_call | solution.py:672
  23.3 4.5 %collective-permute-start.4 = (bf16[4,32,128]{2,1,0:T(8,128)(2,1)S(1)}, bf16[4,32,128]{2,1,0:T(8,128)(2,1)S(1)}, u32[]{:S(2)}, u32[]{:S(2)}) collective-permute-start(bf16[4,32,128]{2,1,0:T(8,128)(2,1)S(1)} %get-tuple-element.26), channel_id=1, source_target_pairs={{0,1},{1,2},{2,3},{3,4},{4,5},{5,6},{6,7},{7,8},{8,9},{9,10},{10,1... | collective-permute-start | bytes 98312 | tf_op jit(solution)/shard_map/ppermute | solution.py:689
  27.8 1.3 %collective-permute-start.5 = (bf16[4,32,128]{2,1,0:T(8,128)(2,1)S(1)}, bf16[4,32,128]{2,1,0:T(8,128)(2,1)S(1)}, u32[]{:S(2)}, u32[]{:S(2)}) collective-permute-start(bf16[4,32,128]{2,1,0:T(8,128)(2,1)S(1)} %get-tuple-element.27), channel_id=1, source_target_pairs={{1,0},{2,1},{3,2},{4,3},{5,4},{6,5},{7,6},{8,7},{9,8},{10,9},{11,1... | collective-permute-start | bytes 98312 | tf_op jit(solution)/shard_map/ppermute | solution.py:690
  29.1 0.0 collective-permute-done.4.below_ref
  29.2 1.8 %collective-permute-done.5.above_ref = bf16[4,32,128]{2,1,0:T(8,128)(2,1)S(1)} collective-permute-done((bf16[4,32,128]{2,1,0:T(8,128)(2,1)S(1)}, bf16[4,32,128]{2,1,0:T(8,128)(2,1)S(1)}, u32[]{:S(2)}, u32[]{:S(2)}) %collective-permute-start.5) | collective-permute-done | bytes 32800 | tf_op jit(solution)/shard_map/ppermute | solution.py:690
  30.9 8.5 %shard_map.88 = f32[1536,128]{1,0:T(8,128)S(1)} custom-call(s32[4,16]{1,0:T(4,128)S(1)} %add_add_fusion.meta, f32[4,16,16,128]{3,2,1,0:T(8,128)S(1)} %get-tuple-element.24.cot_ref, f32[4,18,32,128]{3,2,1,0:T(8,128)S(1)} %get-tuple-element.25.ext_in, bf16[4,32,128]{2,1,0:T(8,128)(2,1)S(1)} %collective-permute-done.4.below_ref, ...), custom_call_target="tpu_custom_call" | custom-call | tf_op jit(solution)/shard_map/pallas_call | solution.py:691
  39.4 25.8 %shard_map.89 = (f32[27,128]{1,0:T(8,128)S(1)}, f32[27,64]{1,0:T(8,128)S(1)}) custom-call(f32[16,2,48,128]{3,2,1,0:T(8,128)S(1)} %bitcast.8), custom_call_target="tpu_custom_call" | custom-call | tf_op jit(solution)/shard_map/pallas_call | solution.py:712
  65.3 0.6 copy.13
  65.9 0.6 copy.14
  (1 shorter events, 0.0 us)
Async XLA Ops:
  0.6 4.4 %copy-start.5 = (s32[1,1,4,6]{3,2,1,0:T(4,128)S(1)}, s32[1,1,4,6]{3,2,1,0:T(4,128)}, u32[]{:S(2)}) copy-start(s32[1,1,4,6]{3,2,1,0:T(4,128)} %param.10) | copy-start | bytes 292
  1.4 3.7 %collective-permute-start = (s32[4,2]{1,0:T(4,128)S(1)}, s32[4,2]{1,0:T(4,128)S(1)}, u32[]{:S(2)}, u32[]{:S(2)}) collective-permute-start(s32[4,2]{1,0:T(4,128)S(1)} %copy.10), channel_id=1, source_target_pairs={{0,1},{1,0},{2,3},{3,2},{4,5},{5,4},{6,7},{7,6},{8,9},{9,8},{10,11... | collective-permute-start | bytes 104 | tf_op jit(solution)/shard_map/ppermute | solution.py:636
  1.4 1.6 %copy-start = (bf16[1,1,4,16,16,1024]{5,4,3,2,1,0:T(8,128)(2,1)S(1)}, bf16[1,1,4,16,16,1024]{5,4,3,2,1,0:T(8,128)(2,1)}, u32[]{:S(2)}) copy-start(bf16[1,1,4,16,16,1024]{5,4,3,2,1,0:T(8,128)(2,1)} %param.7) | copy-start | bytes 6291460
  3.0 1.3 %copy-start.4 = (bf16[27,64]{1,0:T(8,128)(2,1)S(1)}, bf16[27,64]{1,0:T(8,128)(2,1)}, u32[]{:S(2)}) copy-start(bf16[27,64]{1,0:T(8,128)(2,1)} %param.12) | copy-start | bytes 10372
  3.0 1.3 %copy-start.3 = (bf16[27,4096]{1,0:T(8,128)(2,1)S(1)}, bf16[27,4096]{1,0:T(8,128)(2,1)}, u32[]{:S(2)}) copy-start(bf16[27,4096]{1,0:T(8,128)(2,1)} %param.11) | copy-start | bytes 663556
  3.6 1.6 %collective-permute-start.1 = (bf16[32,512]{1,0:T(8,128)(2,1)S(1)}, bf16[32,512]{1,0:T(8,128)(2,1)S(1)}, u32[]{:S(2)}, u32[]{:S(2)}) collective-permute-start(bf16[32,512]{1,0:T(8,128)(2,1)S(1)} %get-tuple-element.19), channel_id=1, source_target_pairs={{0,1},{1,0},{2,3},{3,2},{4,5},{5,4},{6,7},{7,6},{8,9},{9,8},{10,11... | collective-permute-start | bytes 98312 | tf_op jit(solution)/shard_map/ppermute | solution.py:648
  4.8 14.2 %copy-start.2 = (f32[1,1,4,16,256]{4,3,2,1,0:T(8,128)S(1)}, f32[1,1,4,16,256]{4,3,2,1,0:T(8,128)}, u32[]{:S(2)}) copy-start(f32[1,1,4,16,256]{4,3,2,1,0:T(8,128)} %param.8) | copy-start | bytes 196612
  11.4 1.3 %copy-start.1 = (bf16[4,16,16,1024]{3,2,1,0:T(8,128)(2,1)}, bf16[4,16,16,1024]{3,2,1,0:T(8,128)(2,1)S(1)}, u32[]{:S(2)}) copy-start(bf16[4,16,16,1024]{3,2,1,0:T(8,128)(2,1)S(1)} %get-tuple-element.28.mixed_ref) | copy-start | bytes 6291460
  12.8 3.4 %collective-permute-start.2 = (f32[4,16,128]{2,1,0:T(8,128)S(1)}, f32[4,16,128]{2,1,0:T(8,128)S(1)}, u32[]{:S(2)}, u32[]{:S(2)}) collective-permute-start(f32[4,16,128]{2,1,0:T(8,128)S(1)} %get-tuple-element.21), channel_id=1, source_target_pairs={{0,1},{1,2},{2,3},{3,4},{4,5},{5,6},{6,7},{7,8},{8,9},{9,10},{10,1... | collective-permute-start | bytes 98312 | tf_op jit(solution)/shard_map/ppermute | solution.py:670
  14.9 4.2 %collective-permute-start.3 = (f32[4,16,128]{2,1,0:T(8,128)S(1)}, f32[4,16,128]{2,1,0:T(8,128)S(1)}, u32[]{:S(2)}, u32[]{:S(2)}) collective-permute-start(f32[4,16,128]{2,1,0:T(8,128)S(1)} %get-tuple-element.22), channel_id=1, source_target_pairs={{1,0},{2,1},{3,2},{4,3},{5,4},{6,5},{7,6},{8,7},{9,8},{10,9},{11,1... | collective-permute-start | bytes 98312 | tf_op jit(solution)/shard_map/ppermute | solution.py:671
  23.3 5.8 %collective-permute-start.4 = (bf16[4,32,128]{2,1,0:T(8,128)(2,1)S(1)}, bf16[4,32,128]{2,1,0:T(8,128)(2,1)S(1)}, u32[]{:S(2)}, u32[]{:S(2)}) collective-permute-start(bf16[4,32,128]{2,1,0:T(8,128)(2,1)S(1)} %get-tuple-element.26), channel_id=1, source_target_pairs={{0,1},{1,2},{2,3},{3,4},{4,5},{5,6},{6,7},{7,8},{8,9},{9,10},{10,1... | collective-permute-start | bytes 98312 | tf_op jit(solution)/shard_map/ppermute | solution.py:689
  27.8 3.1 %collective-permute-start.5 = (bf16[4,32,128]{2,1,0:T(8,128)(2,1)S(1)}, bf16[4,32,128]{2,1,0:T(8,128)(2,1)S(1)}, u32[]{:S(2)}, u32[]{:S(2)}) collective-permute-start(bf16[4,32,128]{2,1,0:T(8,128)(2,1)S(1)} %get-tuple-element.27), channel_id=1, source_target_pairs={{1,0},{2,1},{3,2},{4,3},{5,4},{6,5},{7,6},{8,7},{9,8},{10,9},{11,1... | collective-permute-start | bytes 98312 | tf_op jit(solution)/shard_map/ppermute | solution.py:690

commit v3 on v1

v3 whole, which is shorter than its diff:
```python
import jax
import jax.numpy as jnp
from jax import lax
from jax.experimental import pallas as pl
from jax.experimental.pallas import tpu as pltpu
from jax.sharding import PartitionSpec as P

F32 = jnp.float32
BF16 = jnp.bfloat16
VM = pl.BlockSpec(memory_space=pltpu.VMEM)
SM = pl.BlockSpec(memory_space=pltpu.SMEM)
B = 4


def iota(shape, dim):
    return lax.broadcasted_iota(jnp.int32, shape, dim)


def repeat(count, body, step):
    def some(i, unused):
        for k in range(step):
            body(i * step + k)
        return unused

    if step == count:
        some(0, 0)
    else:
        lax.fori_loop(0, count // step, some, 0)


def lane_roll(v, shift):
    return pltpu.roll(v, shift % 128, v.ndim - 1)


def group_at(dz, dy):
    if dz == 0:
        return 24 * dy
    if dz == 2:
        return 128 + 24 * dy
    return 72 + 24 * dy if dy < 2 else 128 + 72


def pool_phase(feat_ref, pooled_ref):
    row, col = iota((64, 256), 0), iota((64, 256), 1)
    hit = (row // 8 == col // 32) & (row % 8 == (col % 16) // 2)
    gather = jnp.where(hit, 0.125, 0.0).astype(BF16)
    low = iota((64, 128), 1) < 64
    for b in range(B):
        rows = jnp.dot(gather, feat_ref[b].reshape(256, 1024), preferred_element_type=F32)
        for p in range(4):
            first = rows[:, 256 * p : 256 * p + 128]
            second = rows[:, 256 * p + 128 : 256 * p + 256]
            both = jnp.where(low, first + lane_roll(first, 64), second + lane_roll(second, 64))
            both = both.astype(BF16).astype(F32)
            for z in range(8):
                pooled_ref[z, 8 * b : 8 * b + 8, 128 * p : 128 * p + 128] = both[8 * z : 8 * z + 8]


def coarse_weights(wide_ref, band_ref):
    low = iota((64, 128), 1) < 64
    zero = jnp.zeros((64, 128), F32)
    for k in range(9):
        taps = [wide_ref[3 * k + dx].astype(F32) for dx in range(3)]
        for t in range(2):
            for kx in range(8):
                d0 = kx - 1 - 2 * t
                d1 = d0 - 1
                v0 = taps[d0] if 0 <= d0 < 3 else zero
                v1 = taps[d1] if 0 <= d1 < 3 else zero
                band_ref[k, 64 * kx : 64 * kx + 64, 128 * t : 128 * t + 128] = jnp.where(
                    low, v0, v1
                ).astype(BF16)


def pick(link, slots, load):
    v = None
    for a in slots:
        hit = link == a if not isinstance(link, list) else link[a]
        got = load(a)
        v = jnp.where(hit, got, jnp.zeros_like(got) if v is None else v)
    return v


def others(b):
    return [a for a in range(B) if a != b]


def framer(meta, col):
    row = iota((8, 768), 0)

    def masked(cond, v):
        return jnp.where(cond, v, jnp.zeros_like(v))

    def roles(b):
        bx, by = meta[b, 0], meta[b, 1]
        found = {key: [] for key in ((0, 0), (0, 1), (1, 0), (1, 1))}
        for a in range(B):
            ax, ay = meta[a, col], meta[a, col + 1]
            same = (ax >= 0) & (bx >= 0) & ((ax >> 1) == (bx >> 1)) & ((ay >> 1) == (by >> 1))
            for key in found:
                found[key].append(same & ((ax != bx) == bool(key[0])) & ((ay != by) == bool(key[1])))
        return found

    def rows_of(view, who, b):
        xh, yh = meta[b, 0] & 1, meta[b, 1] & 1

        def take(key, lo, hi):
            if col == 0:
                slots = [b] if key == (0, 0) else others(b)
            else:
                slots = list(range(B))
            return pick(who[key], slots, lambda a: view(slice(8 * a, 8 * a + 8), slice(lo, hi)))

        def wide(mid, side):
            return jnp.concatenate(
                [
                    masked(xh == 1, take(side, 384, 512)),
                    take(mid, 0, 512),
                    masked(xh == 0, take(side, 0, 128)),
                ],
                axis=1,
            )

        own = wide((0, 0), (1, 0))
        near = wide((0, 1), (1, 1))
        before = jnp.where(row == 0, masked(yh == 1, pltpu.roll(near, 1, 0)), pltpu.roll(own, 1, 0))
        after = jnp.where(row == 7, masked(yh == 0, pltpu.roll(near, 7, 0)), pltpu.roll(own, 7, 0))
        return before, own, after

    return masked, [roles(b) for b in range(B)], rows_of


def frame_coarse(meta, pooled_ref, frame_ref):
    masked, roles, rows_of = framer(meta, 0)

    def one_plane(z):
        for q in range(2):
            pair = [rows_of(lambda r, c: pooled_ref[z, r, c], roles[b], b) for b in (2 * q, 2 * q + 1)]
            for dy in range(3):
                frame_ref[dy, z + 1, 16 * q : 16 * q + 16, :] = jnp.concatenate(
                    [pair[0][dy], pair[1][dy]], axis=0
                ).astype(BF16)

    repeat(8, one_plane, 2)


def frame_sibling(meta, sib_ref, frame_ref, zh):
    masked, roles, rows_of = framer(meta, 2)
    for q in range(2):
        pair = [rows_of(lambda r, c: sib_ref[r, c], roles[b], b) for b in (2 * q, 2 * q + 1)]
        for dy in range(3):
            both = jnp.concatenate([pair[0][dy], pair[1][dy]], axis=0)
            frame_ref[dy, 0, 16 * q : 16 * q + 16, :] = masked(zh == 1, both).astype(BF16)
            frame_ref[dy, 9, 16 * q : 16 * q + 16, :] = masked(zh == 0, both).astype(BF16)


def coarse_conv(frame_ref, band_ref, pre_ref):
    for h in range(2):
        total = None
        for dz in range(3):
            for dy in range(3):
                lhs = frame_ref[dy, dz : dz + 8, :, 256 * h : 256 * h + 512].reshape(256, 512)
                term = jnp.dot(lhs, band_ref[3 * dz + dy], preferred_element_type=F32)
                total = term if total is None else total + term
        pre_ref[:, :, 256 * h : 256 * h + 256] = total.reshape(8, 32, 256)


def mix_phase(meta, feat_ref, pre_ref, up_ref, mixed_ref, planes):
    low = iota((8, 128), 1) < 64

    def one(zc):
        for b in range(B):
            alive = meta[b, 0] >= 0
            for p in range(4):
                v = pre_ref[zc, 8 * b : 8 * b + 8, 128 * p : 128 * p + 128]
                v = jnp.maximum(v, 0.0).astype(BF16).astype(F32)
                turned = lane_roll(v, 64)
                for half in range(2):
                    d = jnp.where(low, v, turned) if half == 0 else jnp.where(low, turned, v)
                    for r in range(2):
                        up_ref[8 * b + 2 * p + half, pl.ds(r, 8, stride=2), :] = d
            for l in range(8):
                u = up_ref[8 * b + l]
                for r in range(2):
                    f = feat_ref[b, 2 * zc + r, :, 128 * l : 128 * l + 128].astype(F32)
                    m = jnp.where(alive, f + u, 0.0)
                    mixed_ref[b, 2 * zc + r, :, 128 * l : 128 * l + 128] = m.astype(BF16)

    for zc in planes:
        one(zc)


def decoder_bands(wdec_ref, bandt_ref):
    xi = iota((24, 128), 0)
    half = iota((24, 128), 1) // 64
    bandt_ref[...] = jnp.zeros_like(bandt_ref)
    for dz in range(3):
        for dy in range(3):
            taps = [
                jnp.broadcast_to(wdec_ref[9 * dz + 3 * dy + dx : 9 * dz + 3 * dy + dx + 1, :], (24, 128))
                for dx in range(3)
            ]
            at = group_at(dz, dy)
            for l in range(8):
                x = 2 * l + half
                v = jnp.zeros((24, 128), F32)
                for dx in range(3):
                    v = jnp.where(xi == x - dx + 2, taps[dx], v)
                bandt_ref[at : at + 24, 128 * l : 128 * l + 128] = v


def edge_phase(mixed_ref, bandb_ref, edge_ref):
    for side, z, at in ((0, 15, 0), (1, 0, 128)):
        edge = lax.dot_general(
            mixed_ref[:, z].reshape(64, 1024),
            bandb_ref[at : at + 128, :],
            (((1,), (1,)), ((), ())),
            preferred_element_type=F32,
        )
        edge_ref[side] = edge.reshape(B, 16, 128)


def decode_phase(mixed_ref, bandb_ref, tiles_ref, part_ref):
    lane = iota((16, 128), 1)
    bandt = bandb_ref[...]
    for b in range(B):
        tiles = lax.dot_general(
            mixed_ref[b].reshape(256, 1024),
            bandt,
            (((1,), (1,)), ((), ())),
            preferred_element_type=F32,
        )
        tiles_ref[...] = tiles.reshape(16, 16, 256)
        for z in range(16):
            t0, t1 = tiles_ref[z, :, 0:128], tiles_ref[z, :, 128:256]
            v = jnp.where(lane < 48, lane_roll(t0, -72), lane_roll(t1, -24))
            if z > 0:
                v = v + tiles_ref[z - 1, :, 0:128]
            if z < 15:
                v = v + tiles_ref[z + 1, :, 128:256]
            part_ref[256 * b + 16 * z : 256 * b + 16 * z + 16, :] = v


def target_phase(target_ref, wide_ref):
    for y in range(16):
        j, k = y // 8, y % 8
        v = target_ref[:, 128 * j : 128 * j + 128]
        wide_ref[pl.ds(y, 64, stride=16), :] = lane_roll(v, 1 - 16 * k)


def each(planes, body):
    if isinstance(planes, list):
        for z in planes:
            body(z)
    else:
        first, count, step = planes
        repeat(count, lambda i: body(first + i), step)


def plane_at(b, z):
    at = 256 * b + 16 * z
    return pl.ds(at if isinstance(at, int) else pl.multiple_of(at, 16), 16)


def tall_at(b, z, row, rows):
    at = 32 * (18 * b + z) + row
    return pl.ds(at if isinstance(at, int) else pl.multiple_of(at, 8), rows)


def receive_edges(meta, part_ref, edge_ref):
    for b in range(B):
        for i, z in ((0, 0), (1, 15)):
            got = pick(meta[b, 4 + i], range(B), lambda a: edge_ref[i, a])
            part_ref[plane_at(b, z), :] = part_ref[plane_at(b, z), :] + got


def predict_y(meta, part_ref, halo_ref, sum_ref, planes):
    row = iota((16, 128), 0)
    for b in range(B):
        for i, y in ((0, 15), (1, 0)):
            halo_ref[2 * b + i] = pick(
                meta[b, 6 + i], others(b), lambda a: part_ref[pl.ds(256 * a + y, 16, stride=16), :]
            )
    for b in range(B):

        def along_y(z, b=b):
            own = part_ref[plane_at(b, z), :]
            low = jnp.broadcast_to(halo_ref[2 * b, pl.ds(z, 1), :], (16, 128))
            high = jnp.broadcast_to(halo_ref[2 * b + 1, pl.ds(z, 1), :], (16, 128))
            d0 = jnp.where(row == 0, low, pltpu.roll(own, 1, 0))
            d2 = jnp.where(row == 15, high, pltpu.roll(own, 15, 0))
            sum_ref[plane_at(b, z), :] = d0 + lane_roll(own, -24) + lane_roll(d2, -48)

        each(planes, along_y)


def predict_x(meta, sum_ref, wide_ref, res_ref, cot_ref, planes):
    lane = iota((16, 128), 1)
    for b in range(B):

        def along_x(z, b=b):
            at = plane_at(b, z)
            own = sum_ref[at, :]
            low, high = (
                pick(meta[b, 8 + i], others(b), lambda a: sum_ref[plane_at(a, z), :]) for i in range(2)
            )
            own = own + jnp.where(lane == 1, lane_roll(low, -16), 0.0)
            own = own + jnp.where(lane == 16, lane_roll(high, 16), 0.0)
            keep = (lane >= 1) & (lane <= 16) & (meta[b, 0] >= 0)
            res = jnp.where(keep, own - wide_ref[at, :], 0.0)
            res_ref[at, :] = res
            cot_ref[at, :] = (res * (1.0 / 16384)).astype(BF16).astype(F32)

        each(planes, along_x)


def residual_out(res_ref, out_ref):
    group = iota((64, 128), 1) // 16
    for j in range(2):
        v = jnp.zeros((64, 128), F32)
        for k in range(8):
            got = lane_roll(res_ref[pl.ds(8 * j + k, 64, stride=16), :], 16 * k - 1)
            v = jnp.where(group == k, got, v)
        out_ref[:, 128 * j : 128 * j + 128] = v


def spread_x(own, low, high):
    lane = iota(own.shape, 1)
    own = jnp.where(lane == 0, lane_roll(low, -16), own)
    return jnp.where(lane == 17, lane_roll(high, 16), own)


def sides_of(meta, b, load):
    return load(b), *(pick(meta[b, 8 + i], others(b), load) for i in range(2))


ROWS = ((0, 7, 23, 15), (1, 24, 8, 0))


def extend_phase(meta, cot_ref, ext_ref, full_ref, planes):
    for b in range(B):

        def along_x(z, b=b):
            v = spread_x(*sides_of(meta, b, lambda a: cot_ref[plane_at(a, z), :]))
            ext_ref[tall_at(b, z + 1, 8, 16), :] = v
            full_ref[tall_at(b, z + 1, 8, 16), :] = v

        each(planes, along_x)


def extend_rows(meta, ext_ref, spans):
    for b in range(B):
        for i, row, source, _ in ROWS:
            for z, count in spans:
                ext_ref[pl.ds(32 * (18 * b + z) + row, count, stride=32), :] = pick(
                    meta[b, 6 + i],
                    others(b),
                    lambda a: ext_ref[pl.ds(32 * (18 * a + z) + source, count, stride=32), :],
                )


def full_rows(meta, cot_ref, halo_ref, full_ref):
    for b in range(B):
        for i, _, _, y in ROWS:
            halo_ref[2 * b + i] = pick(
                meta[b, 6 + i], others(b), lambda a: cot_ref[pl.ds(256 * a + y, 16, stride=16), :]
            )
    for b in range(B):
        for i, row, _, _ in ROWS:
            v = spread_x(*sides_of(meta, b, lambda a: halo_ref[2 * a + i]))
            full_ref[pl.ds(32 * (18 * b + 1) + row, 16, stride=32), :] = v


def full_edges(meta, cot_in, rim_ref, line_ref, full_ref):
    lane = iota((16, 128), 1)
    for b in range(B):
        for i in range(2):
            got = pick(meta[b, 4 + i], range(B), lambda a: cot_in[i, a].astype(F32))[8:24]
            rim_ref[i, b] = jnp.where((lane >= 1) & (lane <= 16), got, 0.0)
    for b in range(B):
        for i, z in ((0, 0), (1, 17)):
            v = spread_x(*sides_of(meta, b, lambda a: rim_ref[i, a]))
            full_ref[tall_at(b, z, 8, 16), :] = v
            for k, _, _, y in ROWS:
                line_ref[2 * i + k, 8 * b : 8 * b + 8, :] = jnp.broadcast_to(
                    pick(meta[b, 6 + k], others(b), lambda a: rim_ref[i, a, y : y + 1, :]), (8, 128)
                )
    for b in range(B):
        for i, z in ((0, 0), (1, 17)):
            for k, row, _, _ in ROWS:
                v = spread_x(*sides_of(meta, b, lambda a: line_ref[2 * i + k, 8 * a : 8 * a + 8, :]))
                full_ref[tall_at(b, z, row, 1), :] = v[0:1]


def adjoint_taps(ext_ref, taps_ref, planes):
    lane = iota((16, 128), 1)
    for b in range(B):

        def gather(z, b=b):
            s0, s1, s2 = (ext_ref[pl.ds(32 * (18 * b + z) + 9 - dy, 16), :] for dy in range(3))
            taps_ref[b, z] = jnp.where(
                lane < 24, s0, jnp.where(lane < 48, lane_roll(s1, 24), lane_roll(s2, 48))
            )

        each(planes, gather)


def adjoint_place(taps_ref, cat_ref, planes):
    lane = iota((16, 128), 1)
    for b in range(B):

        def place(z, b=b):
            mid = taps_ref[b, z + 1]
            t0 = jnp.where(lane < 72, taps_ref[b, z + 2], lane_roll(mid, 72))
            t1 = jnp.where(lane < 72, taps_ref[b, z], lane_roll(mid, 24))
            cat_ref[b, z] = jnp.concatenate([t0, t1], axis=1).astype(BF16)

        each(planes, place)


def decoder_grad(cat_ref, mixed_ref, cross_ref, out_ref):
    cross_ref[...] = lax.dot_general(
        cat_ref[...].reshape(1024, 256),
        mixed_ref[...].reshape(1024, 1024),
        (((0,), (0,)), ((), ())),
        preferred_element_type=F32,
    )
    xi = iota((24, 128), 0)
    half = iota((24, 128), 1) // 64
    for dz in range(3):
        for dy in range(3):
            at = group_at(dz, dy)
            sums = [jnp.zeros((24, 128), F32) for _ in range(3)]
            for l in range(8):
                v = cross_ref[at : at + 24, 128 * l : 128 * l + 128]
                for dx in range(3):
                    sums[dx] = sums[dx] + jnp.where(xi == 2 * l + half - dx + 2, v, 0.0)
            for dx in range(3):
                line = jnp.sum(sums[dx], axis=0, keepdims=True)
                line = line + lane_roll(line, 64)
                tap = 9 * dz + 3 * dy + dx
                out_ref[tap : tap + 1, :] = line


def spread_gather(full_ref, lhs_ref, planes):
    group = iota((8, 128), 1) // 32
    for z in planes:
        got = []
        for b in range(B):
            v = full_ref[pl.ds(32 * (18 * b + z) + 7, 8, stride=2), :]
            for j in range(1, 4):
                turned = lane_roll(full_ref[pl.ds(32 * (18 * b + z) + 7 + j, 8, stride=2), :], 32 * j)
                v = jnp.where(group == j, turned, v)
            got.append(v)
        p = jnp.concatenate(got, axis=0).astype(BF16)
        for i in range(z % 2, 4, 2):
            zc = (z - i) // 2
            if 0 <= zc < 8:
                lhs_ref[zc, :, 128 * i : 128 * i + 128] = p


def spread_weights(wdec_ref, high_ref, low_ref):
    row, col = iota((64, 32), 0), iota((64, 32), 1)

    def pick(k, d):
        return ((k == 2 - d) | (k == 3 - d)).astype(F32)

    sel = pick(row // 16, col // 9) * pick((row // 4) % 4, (col // 3) % 3) * pick(row % 4, col % 3)
    sel = jnp.where(col < 27, sel, 0.0).astype(BF16)
    summed = jnp.dot(sel, wdec_ref[...].astype(BF16), preferred_element_type=F32)
    x = iota((32, 128), 0)
    half = iota((32, 128), 1) // 64
    for ij in range(16):
        taps = [jnp.broadcast_to(summed[4 * ij + k : 4 * ij + k + 1, :], (32, 128)) for k in range(4)]
        for t in range(4):
            v = jnp.zeros((32, 128), F32)
            for k in range(4):
                v = jnp.where(x - 2 * (2 * t + half) == k, taps[k], v)
            hi = v.astype(BF16)
            high_ref[32 * ij : 32 * ij + 32, 128 * t : 128 * t + 128] = hi
            low_ref[32 * ij : 32 * ij + 32, 128 * t : 128 * t + 128] = (v - hi.astype(F32)).astype(BF16)


def dpre_phase(meta, lhs_ref, high_ref, low_ref, pre_ref, dpre_ref):
    lhs = lhs_ref[...].reshape(256, 512)
    up = jnp.dot(lhs, high_ref[...], preferred_element_type=F32)
    up = up + jnp.dot(lhs, low_ref[...], preferred_element_type=F32)
    up = up.astype(BF16).astype(F32).reshape(8, 32, 512)
    for b in range(B):
        mine = up[:, 8 * b : 8 * b + 8]
        keep = (pre_ref[:, 8 * b : 8 * b + 8] > 0) & (meta[b, 0] >= 0)
        dpre_ref[:, 8 * b : 8 * b + 8] = jnp.where(keep, mine, 0.0)


def turned_halves(dpre_ref):
    dpre = dpre_ref[...].reshape(256, 512)
    return [dpre[:, 256 * h : 256 * h + 256].T.astype(BF16) for h in range(2)]


def coarse_grad(turned, frame_ref, cross_ref, turn_ref, out_ref, dz):
    low = iota((64, 128), 1) < 64
    low16 = iota((16, 128), 1) < 64
    pending = []
    for dy in range(3):
        total = None
        for h in range(2):
            rhs = frame_ref[dy, dz : dz + 8, :, 256 * h : 256 * h + 512].reshape(256, 512)
            term = jnp.dot(turned[h], rhs, preferred_element_type=F32)
            total = term if total is None else total + term
        cross_ref[dy] = total
        for dx in range(3):
            sums = [None, None]
            for n in range(4):
                m = n + dx + 1
                v = cross_ref[dy, 64 * n : 64 * n + 64, 128 * (m // 2) : 128 * (m // 2) + 128]
                sums[m % 2] = v if sums[m % 2] is None else sums[m % 2] + v
            pending.append((3 * dy + dx, sums[0] + lane_roll(sums[1], 64)))
            if len(pending) == 2 or (dy, dx) == (2, 2):
                slot = pending[0][0] % 4 // 2
                first = pending[0][1]
                second = lane_roll(pending[-1][1], 64)
                turn_ref[slot, :, 0:64] = jnp.where(low, first, second).T
                for i, (row, _) in enumerate(pending):
                    for core in range(2):
                        at = 64 * i + 2 * core
                        even = turn_ref[slot, pl.ds(at, 16, stride=4), :]
                        odd = turn_ref[slot, pl.ds(at + 1, 16, stride=4), :]
                        out_ref[dz, core, pl.ds(row, 16, stride=16), :] = jnp.where(
                            low16, even, lane_roll(odd, 64)
                        )
                pending = []


def decoder_rows(dec_ref, local_ref):
    even = dec_ref[pl.ds(0, 16, stride=2), :]
    odd = dec_ref[pl.ds(1, 16, stride=2), :]
    both = jnp.where(iota((16, 128), 1) < 64, even, odd)
    for g, rows in ((0, jnp.zeros((7, 128), F32)), (1, both[0:7]), (2, both[7:14])):
        for core in range(2):
            for k in range(16):
                local_ref[g, core, 16 * k + 9 : 16 * k + 16, :] = rows


def step_kernel(
    meta, feat_hbm, target_ref, wide_ref, wdec_ref,
    out_ref, coarse_ref, dec_out,
    feat_ref, pooled_ref, plane_ref, sib_in, sib_ref, band_ref, frame_ref, pre_ref, up_ref, mixed_ref,
    bandt_ref, bandb_ref, tiles_ref, part_ref, edge_out, edge_in, cot_out, cot_in, spot_ref, sum_ref,
    cot_ref, res_ref, ext_ref, taps_ref, cat_ref, dcross_ref, halo_ref, rim_ref, line_ref, full_ref, lhs_ref, high_ref,
    low_ref, dpre_ref, cross_ref, turn_ref, dec_ref, local_ref, mate_ref, half_ref, chips_ref, parts_ref,
    feat_sems, sib_sems, edge_sends, edge_recvs, cot_sends, cot_recvs, mate_sends, mate_recvs,
    chip_sends, chip_recvs, dp_sends, dp_recvs,
):
    slab, dp = lax.axis_index("slab"), lax.axis_index("dp")
    count = lax.axis_size("slab")
    core, chip = slab % 2, slab // 2
    chips, copies = count // 2, lax.axis_size("dp")
    sibling = {"slab": slab + 1 - 2 * core}
    around = [{"slab": lax.rem(slab + 1, count)}, {"slab": lax.rem(slab + count - 1, count)}]

    def peer(r):
        return lax.rem(chip + r, chips)

    def twin(r):
        return lax.rem(dp + r, copies)

    def remote(src, dst, send, recv, device):
        return pltpu.make_async_remote_copy(
            src_ref=src,
            dst_ref=dst,
            send_sem=send,
            recv_sem=recv,
            device_id=device,
            device_id_type=pl.DeviceIdType.MESH,
        )

    barrier = pltpu.get_barrier_semaphore()
    greeted = around + [{"slab": 2 * peer(r) + core} for r in range(1, chips)]
    greeted = greeted + [{"dp": twin(r)} for r in range(1, copies)]
    for device in greeted:
        pl.semaphore_signal(barrier, inc=1, device_id=device, device_id_type=pl.DeviceIdType.MESH)

    loads = [
        pltpu.make_async_copy(feat_hbm.at[b], feat_ref.at[b], feat_sems.at[b]) for b in range(B)
    ]
    for load in loads:
        load.start()
    coarse_weights(wide_ref, band_ref)
    for load in loads:
        load.wait()
    pool_phase(feat_ref, pooled_ref)
    plane_ref[...] = pooled_ref[7 * (1 - core)].astype(BF16)
    pl.semaphore_wait(barrier, len(greeted))
    swap = remote(plane_ref, sib_in, sib_sems.at[0], sib_sems.at[1], sibling)
    swap.start()
    frame_coarse(meta, pooled_ref, frame_ref)
    decoder_bands(wdec_ref, bandt_ref)
    bandb_ref[...] = bandt_ref[...].astype(BF16)
    swap.wait()
    sib_ref[...] = sib_in[...].astype(F32)
    frame_sibling(meta, sib_ref, frame_ref, core)
    coarse_conv(frame_ref, band_ref, pre_ref)

    mix_phase(meta, feat_ref, pre_ref, up_ref, mixed_ref, [0, 7])
    edge_phase(mixed_ref, bandb_ref, edge_out)
    edges = [
        remote(edge_out.at[i], edge_in.at[i], edge_sends.at[i], edge_recvs.at[i], around[i])
        for i in range(2)
    ]
    for copy in edges:
        copy.start()
    mix_phase(meta, feat_ref, pre_ref, up_ref, mixed_ref, [1, 2, 3, 4, 5, 6])
    decode_phase(mixed_ref, bandb_ref, tiles_ref, part_ref)
    target_phase(target_ref, spot_ref)
    inner = (1, 14, 7)
    predict_y(meta, part_ref, halo_ref, sum_ref, inner)
    for copy in edges:
        copy.wait()
    receive_edges(meta, part_ref, edge_in)
    predict_y(meta, part_ref, halo_ref, sum_ref, [0, 15])
    predict_x(meta, sum_ref, spot_ref, res_ref, cot_ref, [0, 15])
    extend_phase(meta, cot_ref, ext_ref, full_ref, [0, 15])
    extend_rows(meta, ext_ref, [(1, 1), (16, 1)])
    for b in range(B):
        cot_out[0, b] = ext_ref[tall_at(b, 16, 0, 32), :].astype(BF16)
        cot_out[1, b] = ext_ref[tall_at(b, 1, 0, 32), :].astype(BF16)
    sides = [
        remote(cot_out.at[i], cot_in.at[i], cot_sends.at[i], cot_recvs.at[i], around[i])
        for i in range(2)
    ]
    for copy in sides:
        copy.start()
    predict_x(meta, sum_ref, spot_ref, res_ref, cot_ref, inner)
    extend_phase(meta, cot_ref, ext_ref, full_ref, inner)
    full_rows(meta, cot_ref, halo_ref, full_ref)
    spread_gather(full_ref, lhs_ref, list(range(1, 17)))
    spread_weights(wdec_ref, high_ref, low_ref)
    extend_rows(meta, ext_ref, [(2, 14)])
    adjoint_taps(ext_ref, taps_ref, (1, 16, 8))
    adjoint_place(taps_ref, cat_ref, inner)
    residual_out(res_ref, out_ref)
    for copy in sides:
        copy.wait()
    full_edges(meta, cot_in, rim_ref, line_ref, full_ref)
    spread_gather(full_ref, lhs_ref, [0, 17])
    dpre_phase(meta, lhs_ref, high_ref, low_ref, pre_ref, dpre_ref)
    turned = turned_halves(dpre_ref)

    mates = [
        remote(local_ref.at[g, 1 - core], mate_ref.at[g], mate_sends.at[g], mate_recvs.at[g], sibling)
        for g in range(3)
    ]

    def to_chip(g, r):
        return remote(
            half_ref.at[g, peer(r)], chips_ref.at[g, chip],
            chip_sends.at[g, r], chip_recvs.at[g, chip], {"slab": 2 * peer(r) + core},
        )

    def from_chip(g, r):
        return remote(
            half_ref.at[g, chip], chips_ref.at[g, peer(r)],
            chip_sends.at[g, r], chip_recvs.at[g, peer(r)], {"slab": 2 * peer(r) + core},
        )

    def send_out(g):
        mates[g].wait_recv()
        half_ref[g] = (local_ref[g, core] + mate_ref[g]).reshape(chips, 16, 128)
        for r in range(1, chips):
            to_chip(g, r).start()
        chips_ref[g, chip] = half_ref[g, chip]

    def collect(g):
        for r in range(1, chips):
            from_chip(g, r).wait_recv()
        total = chips_ref[g, 0]
        for k in range(1, chips):
            total = total + chips_ref[g, k]
        parts_ref[dp, 16 * g : 16 * g + 16, :] = total

    for b in range(B):
        for i, z in ((0, 0), (1, 17)):
            got = pick(meta[b, 4 + i], range(B), lambda a: cot_in[i, a].astype(F32))
            ext_ref[tall_at(b, z, 0, 32), :] = got
    adjoint_taps(ext_ref, taps_ref, [0, 17])
    adjoint_place(taps_ref, cat_ref, [0, 15])
    decoder_grad(cat_ref, mixed_ref, dcross_ref, dec_ref)
    decoder_rows(dec_ref, local_ref)
    for g in range(3):
        coarse_grad(turned, frame_ref, cross_ref, turn_ref, local_ref, g)
        mates[g].start()
        if g > 0:
            send_out(g - 1)
    send_out(2)
    for g in range(3):
        collect(g)

    def to_twin(r):
        return remote(
            parts_ref.at[dp], parts_ref.at[dp], dp_sends.at[r], dp_recvs.at[dp], {"dp": twin(r)}
        )

    def from_twin(r):
        return remote(
            parts_ref.at[dp], parts_ref.at[twin(r)], dp_sends.at[r], dp_recvs.at[twin(r)], {"dp": twin(r)}
        )

    for r in range(1, copies):
        to_twin(r).start()
    for r in range(1, copies):
        from_twin(r).wait_recv()
    total = parts_ref[0]
    for k in range(1, copies):
        total = total + parts_ref[k]
    for g in range(3):
        coarse_ref[9 * g : 9 * g + 9, :] = total[16 * g : 16 * g + 9]
    for tap in range(27):
        at = 25 + tap // 2 if tap < 14 else 41 + tap // 2 - 7
        dec_out[tap : tap + 1, :] = total[at : at + 1, 64 * (tap % 2) : 64 * (tap % 2) + 64]
    for g in range(3):
        mates[g].wait_send()
        for r in range(1, chips):
            to_chip(g, r).wait_send()
    for r in range(1, copies):
        to_twin(r).wait_send()


def shape(dims, dtype=F32):
    return jax.ShapeDtypeStruct(dims, dtype)


def per_device(features, target, block_coords, neighbours, owners, coarse_weight, decoder_weight):
    coords = block_coords[0, 0]
    slab, count, copies = lax.axis_index("slab"), lax.axis_size("slab"), lax.axis_size("dp")
    chips = count // 2
    sib_coords = lax.ppermute(coords, "slab", [(i, i ^ 1) for i in range(count)])
    side = jnp.arange(6, dtype=jnp.int32)[None, :]
    outside = ((side == 0) & (slab == 0)) | ((side == 1) & (slab == count - 1))
    links = jnp.where(outside, -1, neighbours[0, 0])
    meta = jnp.concatenate([coords, sib_coords, links], axis=1)
    w3 = coarse_weight.reshape(27, 64, 64)
    wide = jnp.concatenate([w3, w3], axis=2)
    wdec = jnp.pad(
        jnp.concatenate([decoder_weight, decoder_weight], axis=1).astype(F32), ((0, 5), (0, 0))
    )
    scratch = [
        ((B, 16, 16, 1024), BF16),
        ((8, 32, 512), F32),
        ((32, 512), BF16),
        ((32, 512), BF16),
        ((32, 512), F32),
        ((9, 512, 256), BF16),
        ((3, 10, 32, 768), BF16),
        ((8, 32, 512), F32),
        ((32, 16, 128), F32),
        ((B, 16, 16, 1024), BF16),
        ((256, 1024), F32),
        ((256, 1024), BF16),
        ((16, 16, 256), F32),
        ((1024, 128), F32),
        ((2, B, 16, 128), F32),
        ((2, B, 16, 128), F32),
        ((2, B, 32, 128), BF16),
        ((2, B, 32, 128), BF16),
        ((1024, 128), F32),
        ((1024, 128), F32),
        ((1024, 128), F32),
        ((1024, 128), F32),
        ((B * 18 * 32, 128), F32),
        ((B, 18, 16, 128), F32),
        ((B, 16, 16, 256), BF16),
        ((256, 1024), F32),
        ((2 * B, 16, 128), F32),
        ((2, B, 16, 128), F32),
        ((4, 8 * B, 128), F32),
        ((B * 18 * 32, 128), F32),
        ((8, 32, 512), BF16),
        ((512, 512), BF16),
        ((512, 512), BF16),
        ((8, 32, 512), F32),
        ((3, 256, 512), F32),
        ((2, 128, 128), F32),
        ((32, 128), F32),
        ((3, 2, 256, 128), F32),
        ((3, 256, 128), F32),
        ((3, chips, 16, 128), F32),
        ((3, chips, 16, 128), F32),
        ((copies, 48, 128), F32),
    ]
    sems = [(B,), (2,), (2,), (2,), (2,), (2,), (3,), (3,), (3, chips), (3, chips), (copies,), (copies,)]
    res, mine, dec = pl.pallas_call(
        step_kernel,
        in_specs=[SM, pl.BlockSpec(memory_space=pl.ANY), VM, VM, VM],
        out_shape=[shape((64, 256)), shape((27, 128)), shape((27, 64))],
        out_specs=[VM, VM, VM],
        scratch_shapes=[pltpu.VMEM(d, t) for d, t in scratch]
        + [pltpu.SemaphoreType.DMA(d) for d in sems],
        compiler_params=pltpu.CompilerParams(
            collective_id=0, has_side_effects=True, vmem_limit_bytes=48 * 1024 * 1024
        ),
    )(meta, features[0, 0], target[0, 0].reshape(64, 256), wide, wdec)
    return res.reshape(1, 1, B, 16, 256), mine, dec


def solution(mesh):
    placed = (
        P("dp", "slab", None, None, None, None),
        P("dp", "slab", None, None, None),
        P("dp", "slab", None, None),
        P("dp", "slab", None, None),
        P("dp", "slab", None, None),
        P(),
        P(),
    )
    return jax.shard_map(
        per_device,
        mesh=mesh,
        in_specs=placed,
        out_specs=(P("dp", "slab", None, None, None), P(None, "slab"), P()),
        check_vma=False,
    )
```

time: 182 us -> 44.4 us (0.24)
  blocking collectives: 90.5 us -> 0 us
  waiting for transfers between devices: 17.2 us -> 0.01 us
  between operations: 14.2 us -> 0.66 us
  Pallas kernels: 45.4 us -> 35.2 us
  starting transfers between devices: 9.84 us -> 0.01 us
  local copies, waits for them, and re-layouts: 4.22 us -> 6.45 us
    psum x2 -> x0, blocking collectives: 90.5 us -> none  [the longest x1 72.5 us: per_device(): dec = lax.psum(dec[:27, :64], ('dp', 'slab'))]
    reduce_scatter x1 -> x0, waiting for transfers between devices: 12.6 us -> none  [per_device(): lax.psum_scatter(coarse.reshape(32, 32, 128), 'slab', scatter_dimension=0...]
    pallas_call x4 -> x1, Pallas kernels: 45.4 us -> 35.2 us  [per_device(): pl.pallas_call(step_kernel, in_specs=[SM, pl.BlockSpec(memory_space=pl.AN...]
    ppermute x5 -> x0, starting transfers between devices: 9.8 us -> none  [the longest x1 4.52 us: per_device(): cot_below = lax.ppermute(high_plane, 'slab', up)]
    ppermute x5 -> x0, waiting for transfers between devices: 4.64 us -> none  [the longest x1 2.85 us: per_device(): above = lax.ppermute(down_edge, 'slab', down)]
    unnamed x12 -> x7, local copies, waits for them, and re-layouts: 2.94 us -> 4.27 us
  transfers between devices with their start and end apart: 7 -> 1, of which waited for: 3 -> 0; matrix products, arithmetic and copies ran while one was open for 1% -> 7% of each run, Pallas kernels for 0% -> 0%
where the time goes in v3:
time: 44.4 us; the launch traced here: 44.1 us
  Pallas kernels  35.2 us (79%)
  local copies, waits for them, and re-layouts  6.45 us (15%)
  other arithmetic  1.87 us (4%)
  between operations  0.66 us (1%)
    pallas_call x1, Pallas kernels, per_device(): pl.pallas_call(step_kernel, in_specs=[SM, pl.BlockSpec(memory_space=pl.AN...  35.2 us
    unnamed x7, local copies, waits for them, and re-layouts  4.27 us
    reshape x1, local copies, waits for them, and re-layouts, per_device(): w3 = coarse_weight.reshape(27, 64, 64)  1.41 us
  transfers between devices with their start and end apart: 1, of which 0 were waited for; matrix products, arithmetic and copies ran while one was open for 7% of the time, Pallas kernels for 0%

profile of v3, /device:TPU:0, one launch (start us, length us, event | category | flops | bytes accessed | tf_op | source)
XLA Modules:
  0.0 44.1 jit_solution(11508855273946310159)
XLA Ops:
  0.6 0.8 %copy.10 = s32[4,2]{1,0:T(4,128)S(1)} copy(s32[4,2]{0,1:T(2,128)} %bitcast.9) | data formatting | bytes 64 | tf_op jit(solution)/shard_map/squeeze | solution.py:733
  1.4 0.0 collective-permute-start
  1.4 1.4 %reshape.27 = bf16[27,64,64]{2,1,0:T(8,128)(2,1)S(1)} reshape(bf16[27,4096]{1,0:T(8,128)(2,1)} %param.11) | data formatting | bytes 442368 | tf_op jit(solution)/shard_map/reshape | solution.py:741
  2.8 0.2 pad_maximum_fusion.wide_ref
  3.1 0.9 %fusion.3.wdec_ref = f32[32,128]{1,0:T(8,128)S(1)} fusion(bf16[27,64]{1,0:T(8,128)(2,1)} %param.12), kind=kLoop, calls=%fused_computation.5 | loop fusion | flops 28672 | bytes 19840 | tf_op jit(solution)/shard_map/jit(_pad)/pad | solution.py:743
  3.9 0.7 %bitcast_select_fusion = s32[4,6]{1,0:T(4,128)S(1)} fusion(s32[1,1,4,6]{3,2,1,0:T(4,128)} %param.10, pred[6]{0:T(512)(128)(4,1)S(1)} %and_or_fusion), kind=kLoop, calls=%fused_computation.7 | loop fusion | flops 24 | bytes 198 | tf_op jit(solution)/shard_map/jit(_where)/select_n | solution.py:739
  4.6 0.0 collective-permute-done
  4.6 0.1 pad_add_fusion.meta
  4.7 0.0 copy-start
  4.7 1.6 %copy-done = bf16[1,1,4,16,16,1024]{5,4,3,2,1,0:T(8,128)(2,1)S(1)} copy-done((bf16[1,1,4,16,16,1024]{5,4,3,2,1,0:T(8,128)(2,1)S(1)}, bf16[1,1,4,16,16,1024]{5,4,3,2,1,0:T(8,128)(2,1)}, u32[]{:S(2)}) %copy-start) | copy-done | bytes 2097176
  6.3 0.0 copy-start.1
  6.3 0.8 %copy-done.1 = f32[1,1,4,16,256]{4,3,2,1,0:T(8,128)S(1)} copy-done((f32[1,1,4,16,256]{4,3,2,1,0:T(8,128)S(1)}, f32[1,1,4,16,256]{4,3,2,1,0:T(8,128)}, u32[]{:S(2)}) %copy-start.1) | copy-done | bytes 65560
  7.1 35.2 %shard_map.85 = (f32[64,256]{1,0:T(8,128)S(1)}, f32[27,128]{1,0:T(8,128)S(1)}, f32[27,64]{1,0:T(8,128)S(1)}) custom-call(s32[4,10]{1,0:T(4,128)S(1)} %pad_add_fusion.meta, bf16[4,16,16,1024]{3,2,1,0:T(8,128)(2,1)S(1)} %bitcast.6, f32[64,256]{1,0:T(8,128)S(1)} %bitcast.7, bf16[27,64,128]{2,1,0:T(8,128)(2,1)S(1)} %pad_maximum_fusion.wide_ref, ...), custom_call_target="tpu_custom_call" | custom-call | tf_op jit(solution)/shard_map/pallas_call | solution.py:791
  42.3 0.6 %copy.14 = f32[1,1,4,16,256]{4,3,2,1,0:T(8,128)} copy(f32[1,1,4,16,256]{4,3,2,1,0:T(8,128)S(1)} %bitcast.8) | data formatting | bytes 131072
  42.9 0.6 %copy.15 = f32[27,128]{1,0:T(8,128)} copy(f32[27,128]{1,0:T(8,128)S(1)} %get-tuple-element.13) | data formatting | bytes 27648
  43.5 0.6 %copy.16 = f32[27,64]{1,0:T(8,128)} copy(f32[27,64]{1,0:T(8,128)S(1)} %get-tuple-element.14) | data formatting | bytes 13824
  (1 shorter events, 0.0 us)
Async XLA Ops:
  1.4 3.2 %collective-permute-start = (s32[4,2]{1,0:T(4,128)S(1)}, s32[4,2]{1,0:T(4,128)S(1)}, u32[]{:S(2)}, u32[]{:S(2)}) collective-permute-start(s32[4,2]{1,0:T(4,128)S(1)} %copy.10), channel_id=1, source_target_pairs={{0,1},{1,0},{2,3},{3,2},{4,5},{5,4},{6,7},{7,6},{8,9},{9,8},{10,11... | collective-permute-start | bytes 104 | tf_op jit(solution)/shard_map/ppermute | solution.py:736
  4.7 1.6 %copy-start = (bf16[1,1,4,16,16,1024]{5,4,3,2,1,0:T(8,128)(2,1)S(1)}, bf16[1,1,4,16,16,1024]{5,4,3,2,1,0:T(8,128)(2,1)}, u32[]{:S(2)}) copy-start(bf16[1,1,4,16,16,1024]{5,4,3,2,1,0:T(8,128)(2,1)} %param.7) | copy-start | bytes 6291460
  6.3 0.8 %copy-start.1 = (f32[1,1,4,16,256]{4,3,2,1,0:T(8,128)S(1)}, f32[1,1,4,16,256]{4,3,2,1,0:T(8,128)}, u32[]{:S(2)}) copy-start(f32[1,1,4,16,256]{4,3,2,1,0:T(8,128)} %param.8) | copy-start | bytes 196612

commit v4 on v3

--- a/solution.py
+++ b/solution.py
@@ -9,6 +9,7 @@
 BF16 = jnp.bfloat16
 VM = pl.BlockSpec(memory_space=pltpu.VMEM)
 SM = pl.BlockSpec(memory_space=pltpu.SMEM)
+ANY = pl.BlockSpec(memory_space=pl.ANY)
 B = 4
 
 
@@ -40,12 +41,39 @@
     return 72 + 24 * dy if dy < 2 else 128 + 72
 
 
-def pool_phase(feat_ref, pooled_ref):
+class Meta:
+    def __init__(self, coords, links, slab, count):
+        self.coords, self.links = coords, links
+        self.ends = {4: slab == 0, 5: slab == count - 1}
+
+    def __getitem__(self, at):
+        b, col = at
+        if col < 4:
+            return self.coords[col, b]
+        link = self.links[b, col - 4]
+        return jnp.where(self.ends[col], -1, link) if col in self.ends else link
+
+
+def widen_weights(cw_ref, dw_ref, wide_ref, wdec_ref):
+    low = iota((27, 128), 1) < 64
+    for t in range(32):
+        v = cw_ref[:, 128 * t : 128 * t + 128].astype(F32)
+        turned = lane_roll(v, 64)
+        wide_ref[pl.ds(2 * t, 27, stride=64), :] = jnp.where(low, v, turned)
+        wide_ref[pl.ds(2 * t + 1, 27, stride=64), :] = jnp.where(low, turned, v)
+    w = dw_ref[...].astype(F32)
+    wdec_ref[...] = jnp.zeros_like(wdec_ref)
+    wdec_ref[0:27, 0:64] = w
+    wdec_ref[0:27, 64:128] = w
+
+
+def pool_phase(feat_ref, pooled_ref, loads):
     row, col = iota((64, 256), 0), iota((64, 256), 1)
     hit = (row // 8 == col // 32) & (row % 8 == (col % 16) // 2)
     gather = jnp.where(hit, 0.125, 0.0).astype(BF16)
     low = iota((64, 128), 1) < 64
     for b in range(B):
+        loads[b].wait()
         rows = jnp.dot(gather, feat_ref[b].reshape(256, 1024), preferred_element_type=F32)
         for p in range(4):
             first = rows[:, 256 * p : 256 * p + 128]
@@ -60,7 +88,7 @@
     low = iota((64, 128), 1) < 64
     zero = jnp.zeros((64, 128), F32)
     for k in range(9):
-        taps = [wide_ref[3 * k + dx].astype(F32) for dx in range(3)]
+        taps = [wide_ref[64 * (3 * k + dx) : 64 * (3 * k + dx) + 64, :] for dx in range(3)]
         for t in range(2):
             for kx in range(8):
                 d0 = kx - 1 - 2 * t
@@ -85,7 +113,7 @@
     return [a for a in range(B) if a != b]
 
 
-def framer(meta, col):
+def framer(meta, spots=None):
     row = iota((8, 768), 0)
 
     def masked(cond, v):
@@ -95,21 +123,31 @@
         bx, by = meta[b, 0], meta[b, 1]
         found = {key: [] for key in ((0, 0), (0, 1), (1, 0), (1, 1))}
         for a in range(B):
-            ax, ay = meta[a, col], meta[a, col + 1]
+            if spots is None:
+                ax, ay = meta[a, 0], meta[a, 1]
+            else:
+                ax, ay = (
+                    jnp.broadcast_to(spots[B * i + a : B * i + a + 1, :], (8, 128)) for i in range(2)
+                )
             same = (ax >= 0) & (bx >= 0) & ((ax >> 1) == (bx >> 1)) & ((ay >> 1) == (by >> 1))
             for key in found:
-                found[key].append(same & ((ax != bx) == bool(key[0])) & ((ay != by) == bool(key[1])))
+                off_x = ax != bx if key[0] else ax == bx
+                off_y = ay != by if key[1] else ay == by
+                found[key].append(same & off_x & off_y)
         return found
 
     def rows_of(view, who, b):
         xh, yh = meta[b, 0] & 1, meta[b, 1] & 1
 
         def take(key, lo, hi):
-            if col == 0:
+            if spots is None:
                 slots = [b] if key == (0, 0) else others(b)
-            else:
-                slots = list(range(B))
-            return pick(who[key], slots, lambda a: view(slice(8 * a, 8 * a + 8), slice(lo, hi)))
+                return pick(who[key], slots, lambda a: view(slice(8 * a, 8 * a + 8), slice(lo, hi)))
+            parts = [
+                pick(who[key], range(B), lambda a: view(slice(8 * a, 8 * a + 8), slice(at, at + 128)))
+                for at in range(lo, hi, 128)
+            ]
+            return parts[0] if len(parts) == 1 else jnp.concatenate(parts, axis=1)
 
         def wide(mid, side):
             return jnp.concatenate(
@@ -131,7 +169,7 @@
 
 
 def frame_coarse(meta, pooled_ref, frame_ref):
-    masked, roles, rows_of = framer(meta, 0)
+    masked, roles, rows_of = framer(meta)
 
     def one_plane(z):
         for q in range(2):
@@ -144,8 +182,8 @@
     repeat(8, one_plane, 2)
 
 
-def frame_sibling(meta, sib_ref, frame_ref, zh):
-    masked, roles, rows_of = framer(meta, 2)
+def frame_sibling(meta, spots, sib_ref, frame_ref, zh):
+    masked, roles, rows_of = framer(meta, spots)
     for q in range(2):
         pair = [rows_of(lambda r, c: sib_ref[r, c], roles[b], b) for b in (2 * q, 2 * q + 1)]
         for dy in range(3):
@@ -542,19 +580,20 @@
 
 
 def step_kernel(
-    meta, feat_hbm, target_ref, wide_ref, wdec_ref,
+    coords, links, feat_hbm, target_hbm, cw_ref, dw_ref,
     out_ref, coarse_ref, dec_out,
-    feat_ref, pooled_ref, plane_ref, sib_in, sib_ref, band_ref, frame_ref, pre_ref, up_ref, mixed_ref,
+    wide_ref, wdec_ref, target_ref, feat_ref, pooled_ref, spot_out, spot_in, plane_ref, sib_in, sib_ref, band_ref, frame_ref, pre_ref, up_ref, mixed_ref,
     bandt_ref, bandb_ref, tiles_ref, part_ref, edge_out, edge_in, cot_out, cot_in, spot_ref, sum_ref,
     cot_ref, res_ref, ext_ref, taps_ref, cat_ref, dcross_ref, halo_ref, rim_ref, line_ref, full_ref, lhs_ref, high_ref,
     low_ref, dpre_ref, cross_ref, turn_ref, dec_ref, local_ref, mate_ref, half_ref, chips_ref, parts_ref,
-    feat_sems, sib_sems, edge_sends, edge_recvs, cot_sends, cot_recvs, mate_sends, mate_recvs,
+    target_sem, feat_sems, spot_sems, sib_sems, edge_sends, edge_recvs, cot_sends, cot_recvs, mate_sends, mate_recvs,
     chip_sends, chip_recvs, dp_sends, dp_recvs,
 ):
     slab, dp = lax.axis_index("slab"), lax.axis_index("dp")
     count = lax.axis_size("slab")
     core, chip = slab % 2, slab // 2
     chips, copies = count // 2, lax.axis_size("dp")
+    meta = Meta(coords, links, slab, count)
     sibling = {"slab": slab + 1 - 2 * core}
     around = [{"slab": lax.rem(slab + 1, count)}, {"slab": lax.rem(slab + count - 1, count)}]
 
@@ -585,20 +624,31 @@
     ]
     for load in loads:
         load.start()
+    measured = pltpu.make_async_copy(target_hbm, target_ref, target_sem.at[0])
+    measured.start()
+    widen_weights(cw_ref, dw_ref, wide_ref, wdec_ref)
     coarse_weights(wide_ref, band_ref)
-    for load in loads:
-        load.wait()
-    pool_phase(feat_ref, pooled_ref)
+    pool_phase(feat_ref, pooled_ref, loads)
+    line = iota((2 * B, 128), 0)
+    spots = jnp.zeros((2 * B, 128), jnp.int32)
+    for b in range(B):
+        for i in range(2):
+            spots = jnp.where(line == B * i + b, meta[b, i], spots)
+    spot_out[...] = spots
     plane_ref[...] = pooled_ref[7 * (1 - core)].astype(BF16)
     pl.semaphore_wait(barrier, len(greeted))
     swap = remote(plane_ref, sib_in, sib_sems.at[0], sib_sems.at[1], sibling)
     swap.start()
+    places = remote(spot_out, spot_in, spot_sems.at[0], spot_sems.at[1], sibling)
+    places.start()
     frame_coarse(meta, pooled_ref, frame_ref)
+    spread_weights(wdec_ref, high_ref, low_ref)
     decoder_bands(wdec_ref, bandt_ref)
     bandb_ref[...] = bandt_ref[...].astype(BF16)
     swap.wait()
+    places.wait()
     sib_ref[...] = sib_in[...].astype(F32)
-    frame_sibling(meta, sib_ref, frame_ref, core)
+    frame_sibling(meta, spot_in[...], sib_ref, frame_ref, core)
     coarse_conv(frame_ref, band_ref, pre_ref)
 
     mix_phase(meta, feat_ref, pre_ref, up_ref, mixed_ref, [0, 7])
@@ -611,6 +661,7 @@
         copy.start()
     mix_phase(meta, feat_ref, pre_ref, up_ref, mixed_ref, [1, 2, 3, 4, 5, 6])
     decode_phase(mixed_ref, bandb_ref, tiles_ref, part_ref)
+    measured.wait()
     target_phase(target_ref, spot_ref)
     inner = (1, 14, 7)
     predict_y(meta, part_ref, halo_ref, sum_ref, inner)
@@ -634,11 +685,9 @@
     extend_phase(meta, cot_ref, ext_ref, full_ref, inner)
     full_rows(meta, cot_ref, halo_ref, full_ref)
     spread_gather(full_ref, lhs_ref, list(range(1, 17)))
-    spread_weights(wdec_ref, high_ref, low_ref)
     extend_rows(meta, ext_ref, [(2, 14)])
     adjoint_taps(ext_ref, taps_ref, (1, 16, 8))
     adjoint_place(taps_ref, cat_ref, inner)
-    residual_out(res_ref, out_ref)
     for copy in sides:
         copy.wait()
     full_edges(meta, cot_in, rim_ref, line_ref, full_ref)
@@ -692,6 +741,7 @@
         if g > 0:
             send_out(g - 1)
     send_out(2)
+    residual_out(res_ref, out_ref)
     for g in range(3):
         collect(g)
 
@@ -725,27 +775,37 @@
         to_twin(r).wait_send()
 
 
+def hand_out(*refs):
+    count = (len(refs) - 2) // 3
+    ins, outs, held = refs[:count], refs[count : 2 * count], refs[2 * count : 3 * count]
+    in_sems, out_sems = refs[3 * count :]
+    loads = [pltpu.make_async_copy(ins[i], held[i], in_sems.at[i]) for i in range(count)]
+    stores = [pltpu.make_async_copy(held[i], outs[i], out_sems.at[i]) for i in range(count)]
+    for load in loads:
+        load.start()
+    for load, store in zip(loads, stores):
+        load.wait()
+        store.start()
+    for store in stores:
+        store.wait()
+
+
 def shape(dims, dtype=F32):
     return jax.ShapeDtypeStruct(dims, dtype)
 
 
 def per_device(features, target, block_coords, neighbours, owners, coarse_weight, decoder_weight):
-    coords = block_coords[0, 0]
-    slab, count, copies = lax.axis_index("slab"), lax.axis_size("slab"), lax.axis_size("dp")
+    coords = block_coords[0, 0].T
+    count, copies = lax.axis_size("slab"), lax.axis_size("dp")
     chips = count // 2
-    sib_coords = lax.ppermute(coords, "slab", [(i, i ^ 1) for i in range(count)])
-    side = jnp.arange(6, dtype=jnp.int32)[None, :]
-    outside = ((side == 0) & (slab == 0)) | ((side == 1) & (slab == count - 1))
-    links = jnp.where(outside, -1, neighbours[0, 0])
-    meta = jnp.concatenate([coords, sib_coords, links], axis=1)
-    w3 = coarse_weight.reshape(27, 64, 64)
-    wide = jnp.concatenate([w3, w3], axis=2)
-    wdec = jnp.pad(
-        jnp.concatenate([decoder_weight, decoder_weight], axis=1).astype(F32), ((0, 5), (0, 0))
-    )
     scratch = [
+        ((27 * 64, 128), F32),
+        ((32, 128), F32),
+        ((64, 256), F32),
         ((B, 16, 16, 1024), BF16),
         ((8, 32, 512), F32),
+        ((2 * B, 128), jnp.int32),
+        ((2 * B, 128), jnp.int32),
         ((32, 512), BF16),
         ((32, 512), BF16),
         ((32, 512), F32),
@@ -787,18 +847,30 @@
         ((3, chips, 16, 128), F32),
         ((copies, 48, 128), F32),
     ]
-    sems = [(B,), (2,), (2,), (2,), (2,), (2,), (3,), (3,), (3, chips), (3, chips), (copies,), (copies,)]
-    res, mine, dec = pl.pallas_call(
+    sems = [(1,), (B,), (2,), (2,), (2,), (2,), (2,), (2,), (3,), (3,), (3, chips), (3, chips), (copies,), (copies,)]
+    outs = [shape((64, 256)), shape((27, 128)), shape((27, 64))]
+    results = pl.pallas_call(
         step_kernel,
-        in_specs=[SM, pl.BlockSpec(memory_space=pl.ANY), VM, VM, VM],
-        out_shape=[shape((64, 256)), shape((27, 128)), shape((27, 64))],
+        in_specs=[SM] * 2 + [ANY] * 2 + [VM] * 2,
+        out_shape=outs,
         out_specs=[VM, VM, VM],
         scratch_shapes=[pltpu.VMEM(d, t) for d, t in scratch]
         + [pltpu.SemaphoreType.DMA(d) for d in sems],
         compiler_params=pltpu.CompilerParams(
-            collective_id=0, has_side_effects=True, vmem_limit_bytes=48 * 1024 * 1024
+            collective_id=0, has_side_effects=True, vmem_limit_bytes=62 * 1024 * 1024
         ),
-    )(meta, features[0, 0], target[0, 0].reshape(64, 256), wide, wdec)
+    )(
+        coords, neighbours[0, 0], features[0, 0], target[0, 0].reshape(64, 256),
+        coarse_weight, decoder_weight,
+    )
+    res, mine, dec = pl.pallas_call(
+        hand_out,
+        in_specs=[ANY] * 3,
+        out_shape=outs,
+        out_specs=[ANY] * 3,
+        scratch_shapes=[pltpu.VMEM(out.shape, F32) for out in outs]
+        + [pltpu.SemaphoreType.DMA((3,))] * 2,
+    )(*results)
     return res.reshape(1, 1, B, 16, 256), mine, dec
 
 

time: 44.4 us -> 38.7 us (0.87)
  local copies, waits for them, and re-layouts: 6.45 us -> 0 us
  Pallas kernels: 35.2 us -> 37.9 us
  other arithmetic: 1.87 us -> 0 us
    unnamed x7 -> x0, local copies, waits for them, and re-layouts: 4.27 us -> none
    pallas_call x1 -> x2, Pallas kernels: 35.2 us -> 37.9 us  [the longest x1 36.4 us: per_device(): pl.pallas_call(step_kernel, in_specs=[SM] * 2 + [ANY] * 2 + [VM] * 2, out...]
    reshape x1 -> x0, local copies, waits for them, and re-layouts: 1.41 us -> none  [per_device(): w3 = coarse_weight.reshape(27, 64, 64)]
    pad x1 -> x0, other arithmetic: 0.85 us -> none  [per_device(): jnp.pad(jnp.concatenate([decoder_weight, decoder_weight], axis=1).astype(...]
    squeeze x1 -> x0, local copies, waits for them, and re-layouts: 0.77 us -> none  [per_device(): coords = block_coords[0, 0]]
    select_n x1 -> x0, other arithmetic: 0.69 us -> none  [per_device(): links = jnp.where(outside, -1, neighbours[0, 0])]
  transfers between devices with their start and end apart: 1 -> 0, of which waited for: 0 -> 0; matrix products, arithmetic and copies ran while one was open for 7% -> 0% of each run, Pallas kernels for 0% -> 0%
where the time goes in v4:
time: 38.7 us; the launch traced here: 38.5 us
  Pallas kernels  37.9 us (98%)
  between operations  0.64 us (2%)
    pallas_call x1, Pallas kernels, per_device(): pl.pallas_call(step_kernel, in_specs=[SM] * 2 + [ANY] * 2 + [VM] * 2, out...  36.4 us
    pallas_call x1, Pallas kernels, per_device(): pl.pallas_call(hand_out, in_specs=[ANY] * 3, out_shape=outs, out_specs=[A...  1.52 us

profile of v4, /device:TPU:0, one launch (start us, length us, event | category | flops | bytes accessed | tf_op | source)
XLA Modules:
  0.0 38.5 jit_solution(11594117089042686500)
XLA Ops:
  0.6 36.4 %shard_map.85 = (f32[64,256]{1,0:T(8,128)}, f32[27,128]{1,0:T(8,128)}, f32[27,64]{1,0:T(8,128)}) custom-call(s32[2,4]{1,0:T(2,128)} %bitcast.10, s32[4,6]{1,0:T(4,128)} %bitcast.9, bf16[4,16,16,1024]{3,2,1,0:T(8,128)(2,1)} %bitcast.7, f32[64,256]{1,0:T(8,128)} %bitcast.8, bf16[27,4096]{1,0:T(8,128)(2,1)} %cw_ref.1, bf16[27,64]{1,0:T(8,128)(2,1)} %dw_ref.1), custom_call_target="tpu_custom_call" | custom-call | tf_op jit(solution)/shard_map/pallas_call | solution.py:852
  37.0 1.5 %shard_map.86 = (f32[64,256]{1,0:T(8,128)}, f32[27,128]{1,0:T(8,128)}, f32[27,64]{1,0:T(8,128)}) custom-call(f32[64,256]{1,0:T(8,128)} %get-tuple-element.9.refs_0_, f32[27,128]{1,0:T(8,128)} %get-tuple-element.10.refs_1_, f32[27,64]{1,0:T(8,128)} %get-tuple-element.11.refs_2_), custom_call_target="tpu_custom_call" | custom-call | tf_op jit(solution)/shard_map/pallas_call | solution.py:866

commit v5 on v4

--- a/solution.py
+++ b/solution.py
@@ -179,7 +179,7 @@
                     [pair[0][dy], pair[1][dy]], axis=0
                 ).astype(BF16)
 
-    repeat(8, one_plane, 2)
+    repeat(8, one_plane, 4)
 
 
 def frame_sibling(meta, spots, sib_ref, frame_ref, zh):
@@ -663,7 +663,7 @@
     decode_phase(mixed_ref, bandb_ref, tiles_ref, part_ref)
     measured.wait()
     target_phase(target_ref, spot_ref)
-    inner = (1, 14, 7)
+    inner = (1, 14, 14)
     predict_y(meta, part_ref, halo_ref, sum_ref, inner)
     for copy in edges:
         copy.wait()
@@ -686,7 +686,7 @@
     full_rows(meta, cot_ref, halo_ref, full_ref)
     spread_gather(full_ref, lhs_ref, list(range(1, 17)))
     extend_rows(meta, ext_ref, [(2, 14)])
-    adjoint_taps(ext_ref, taps_ref, (1, 16, 8))
+    adjoint_taps(ext_ref, taps_ref, (1, 16, 16))
     adjoint_place(taps_ref, cat_ref, inner)
     for copy in sides:
         copy.wait()

time: 38.7 us -> 38.1 us (0.984)
  Pallas kernels: 37.9 us -> 37.2 us
    pallas_call x1, Pallas kernels: 36.4 us -> 35.7 us  [per_device(): pl.pallas_call(step_kernel, in_specs=[SM] * 2 + [ANY] * 2 + [VM] * 2, out...]
where the time goes in v5:
time: 38.1 us; the launch traced here: 37.9 us
  Pallas kernels  37.2 us (98%)
  between operations  0.64 us (2%)
    pallas_call x1, Pallas kernels, per_device(): pl.pallas_call(step_kernel, in_specs=[SM] * 2 + [ANY] * 2 + [VM] * 2, out...  35.7 us
    pallas_call x1, Pallas kernels, per_device(): pl.pallas_call(hand_out, in_specs=[ANY] * 3, out_shape=outs, out_specs=[A...  1.52 us

profile of v5, /device:TPU:0, one launch (start us, length us, event | category | flops | bytes accessed | tf_op | source)
XLA Modules:
  0.0 37.9 jit_solution(6264863615816408491)
XLA Ops:
  0.6 35.7 %shard_map.85 = (f32[64,256]{1,0:T(8,128)}, f32[27,128]{1,0:T(8,128)}, f32[27,64]{1,0:T(8,128)}) custom-call(s32[2,4]{1,0:T(2,128)} %bitcast.10, s32[4,6]{1,0:T(4,128)} %bitcast.9, bf16[4,16,16,1024]{3,2,1,0:T(8,128)(2,1)} %bitcast.7, f32[64,256]{1,0:T(8,128)} %bitcast.8, bf16[27,4096]{1,0:T(8,128)(2,1)} %cw_ref.1, bf16[27,64]{1,0:T(8,128)(2,1)} %dw_ref.1), custom_call_target="tpu_custom_call" | custom-call | tf_op jit(solution)/shard_map/pallas_call | solution.py:852
  36.3 1.5 %shard_map.86 = (f32[64,256]{1,0:T(8,128)}, f32[27,128]{1,0:T(8,128)}, f32[27,64]{1,0:T(8,128)}) custom-call(f32[64,256]{1,0:T(8,128)} %get-tuple-element.9.refs_0_, f32[27,128]{1,0:T(8,128)} %get-tuple-element.10.refs_1_, f32[27,64]{1,0:T(8,128)} %get-tuple-element.11.refs_2_), custom_call_target="tpu_custom_call" | custom-call | tf_op jit(solution)/shard_map/pallas_call | solution.py:866
